TPU v7x, 128 devices: a whole 4x4x4 slice. The times are simulated.
128 devices in a mesh: lat: 4 (over z), lon: 32 (over x, y, core).
Axes of the slice: x: 4, y: 4, z: 4, core: 2. Of those that a mesh axis runs over, the one named last changes fastest.
Arguments:
- obs_values: bfloat16 [524288, 128], P(('lat', 'lon')), may hold values from -6 to 6
- obs_cells: int32 [524288], P(('lat', 'lon')), may hold values from 0 to 2047
- obs_subcell: int32 [524288], P(('lat', 'lon')), may hold values from 0 to 63
- slot_counts: int32 [128, 128], P(('lat', 'lon')), may hold values from 1 to 32, as said below
- sharpness: float32 [256], replicated, may hold values from 0.3 to 30
- embed_weight: bfloat16 [128, 256], replicated, may hold values from -0.5 to 0.5
- conv_weight: bfloat16 [2, 3, 3, 256, 256], replicated, may hold values from -0.125 to 0.125
- cotangent: bfloat16 [64, 4096, 256], P('lat', 'lon'), may hold values from -6 to 6
Outputs:
- encoded: bfloat16 [64, 4096, 256], P('lat', 'lon')
- value_grads: bfloat16 [524288, 128], P(('lat', 'lon'))
- conv_grads: float32 [2, 3, 3, 256, 256], replicated
- embed_grads: float32 [128, 256], replicated
Inputs may be any that keep to these rules, and one draw needn't show every extreme that they name: `slot_counts`: every source device fills all 32 slots for some destination tile; densities differ by tile.
All inputs are finite; a program needn't handle non-finite values.
Results may differ from a plain program's by a relative error of at most 0.009.
Values may be sent and summed in bfloat16 or wider, within the bound.
A program may use at most 128 MiB of HBM per device.

v0:
```python
import math

import jax
import jax.numpy as jnp
from jax import lax
from jax.sharding import PartitionSpec as P

SUBCELL = 8


def padded_2(block, sides, width, periodic):
    for axis, dim in sides:
        count = lax.axis_size(axis)
        forward = [(i, i + 1) for i in range(count - 1)]
        if periodic:
            forward.append((count - 1, 0))
        backward = [(target, source) for source, target in forward]
        low = lax.ppermute(
            lax.slice_in_dim(block, block.shape[dim] - width, None, axis=dim), axis, forward
        )
        high = lax.ppermute(lax.slice_in_dim(block, 0, width, axis=dim), axis, backward)
        block = jnp.concatenate([low, block, high], axis=dim)
    return block


def widen_tile(field):
    field = padded_2(field, (("lon", 1),), 1, True)
    return padded_2(field, (("lat", 0),), 1, False)


def apply_conv(padded, kernel):
    return lax.conv_general_dilated(
        padded[None],
        kernel,
        (1, 1),
        "VALID",
        dimension_numbers=("NHWC", "HWIO", "NHWC"),
        preferred_element_type=jnp.float32,
    )[0]


def kernel_grad(padded, grad):
    height, breadth = (grad.shape[0], grad.shape[1])
    blocks = []
    for row_off in range(3):
        for col_off in range(3):
            window = padded[row_off : row_off + height, col_off : col_off + breadth]
            blocks.append(
                jnp.einsum("hwc,hwo->co", window, grad, preferred_element_type=jnp.float32)
            )
    return jnp.stack(blocks).reshape(3, 3, padded.shape[2], grad.shape[2])


def flip_kernel(kernel):
    return jnp.flip(kernel, (0, 1)).transpose(0, 1, 3, 2)


def silu_slope(field):
    value = field.astype(jnp.float32)
    sig = jax.nn.sigmoid(value)
    return sig * (1.0 + value * (1.0 - sig))


def on_device(
    obs_values, obs_cells, obs_subcell, slot_counts, sharpness, embed_weight, conv_weight, cotangent
):
    n_lat = lax.axis_size("lat")
    n_lon = lax.axis_size("lon")
    devices = n_lat * n_lon
    slot_cap = obs_values.shape[0] // devices
    val_width = obs_values.shape[1]
    tile_lat, tile_lon, channels = cotangent.shape
    row_count = devices * slot_cap
    values = obs_values.reshape(devices, slot_cap, val_width)
    cell_ids = obs_cells.reshape(devices, slot_cap)
    sub_ids = obs_subcell.reshape(devices, slot_cap)
    live_mask = (
        lax.broadcasted_iota(jnp.int32, (devices, slot_cap), 1) < slot_counts.reshape(devices, 1)
    ).astype(jnp.int32)
    arrived = (
        lax.all_to_all(values, ("lat", "lon"), split_axis=0, concat_axis=0, tiled=True),
        lax.all_to_all(cell_ids, ("lat", "lon"), split_axis=0, concat_axis=0, tiled=True),
        lax.all_to_all(sub_ids, ("lat", "lon"), split_axis=0, concat_axis=0, tiled=True),
        lax.all_to_all(live_mask, ("lat", "lon"), split_axis=0, concat_axis=0, tiled=True),
    )
    recv_values = arrived[0].reshape(row_count, val_width)
    recv_cells = arrived[1].reshape(row_count)
    recv_subs = arrived[2].reshape(row_count)
    recv_live = arrived[3].reshape(row_count)
    off_row = ((recv_subs // SUBCELL).astype(jnp.float32) + 0.5) / SUBCELL - 0.5
    off_col = ((recv_subs % SUBCELL).astype(jnp.float32) + 0.5) / SUBCELL - 0.5
    radius = off_row * off_row + off_col * off_col
    weight = jnp.exp(-radius[:, None] * sharpness[None, :]) * recv_live.astype(jnp.float32)[:, None]
    embedding = jnp.dot(recv_values, embed_weight, preferred_element_type=jnp.float32)
    tile_cells = tile_lat * tile_lon
    placed = jax.ops.segment_sum(embedding * weight, recv_cells, num_segments=tile_cells)
    density = jax.ops.segment_sum(weight, recv_cells, num_segments=tile_cells)
    base_grid = (
        (placed / (density + 1.0)).astype(jnp.bfloat16).reshape(tile_lat, tile_lon, channels)
    )
    act_zero = jax.nn.silu(base_grid.astype(jnp.float32)).astype(jnp.bfloat16)
    pad_zero = widen_tile(act_zero)
    middle = (base_grid.astype(jnp.float32) + apply_conv(pad_zero, conv_weight[0])).astype(
        jnp.bfloat16
    )
    act_one = jax.nn.silu(middle.astype(jnp.float32)).astype(jnp.bfloat16)
    pad_one = widen_tile(act_one)
    encoded = (middle.astype(jnp.float32) + apply_conv(pad_one, conv_weight[1])).astype(
        jnp.bfloat16
    )
    outer = kernel_grad(pad_one, cotangent)
    back_one = apply_conv(widen_tile(cotangent), flip_kernel(conv_weight[1]))
    grad_mid = (cotangent.astype(jnp.float32) + back_one * silu_slope(middle)).astype(jnp.bfloat16)
    inner = kernel_grad(pad_zero, grad_mid)
    back_zero = apply_conv(widen_tile(grad_mid), flip_kernel(conv_weight[0]))
    grad_base = grad_mid.astype(jnp.float32) + back_zero * silu_slope(base_grid)
    grad_placed = grad_base.reshape(tile_cells, channels) / (density + 1.0)
    grad_embed = (weight * jnp.take(grad_placed, recv_cells, axis=0)).astype(jnp.bfloat16)
    grad_vals = lax.dot_general(
        grad_embed, embed_weight, (((1,), (1,)), ((), ())), preferred_element_type=jnp.float32
    ).astype(jnp.bfloat16)
    embed_sum = lax.dot_general(
        recv_values, grad_embed, (((0,), (0,)), ((), ())), preferred_element_type=jnp.float32
    )
    outer_total, inner_total, embed_total = lax.psum((outer, inner, embed_sum), ("lat", "lon"))
    returned = lax.all_to_all(
        grad_vals.reshape(devices, slot_cap, val_width),
        ("lat", "lon"),
        split_axis=0,
        concat_axis=0,
        tiled=True,
    )
    value_grads = returned.reshape(row_count, val_width)
    grad_scale = 1.0 / math.sqrt(tile_lat * n_lat * tile_lon * n_lon)
    conv_grads = jnp.stack([inner_total, outer_total]) * grad_scale
    return (encoded, value_grads, conv_grads, embed_total * grad_scale)


def solution(mesh):
    placed = (
        P(("lat", "lon"), None),
        P(("lat", "lon")),
        P(("lat", "lon")),
        P(("lat", "lon"), None),
        P(),
        P(),
        P(),
        P("lat", "lon", None),
    )
    return jax.shard_map(
        on_device,
        mesh=mesh,
        in_specs=placed,
        out_specs=(P("lat", "lon", None), P(("lat", "lon"), None), P(), P()),
        check_vma=False,
    )
```

profile of v0, /device:TPU:1, one launch (start us, length us, event | category | flops | bytes accessed | tf_op | source)
XLA Modules:
  0.0 491.3 jit_solution(17725453252158403382)
XLA Ops:
  8.2 2.8 collective-permute-start.8
  12.4 10.6 %all-to-all-start = ((s32[128,1,32]{2,1,0:T(1,128)}), s32[128,1,32]{2,1,0:T(1,128)S(1)}, u32[]{:S(2)}, u32[]{:S(2)}) async-start(s32[128,1,32]{2,1,0:T(1,128)} %bitcast), calls=%async_computation | async-start | bytes 131072 | tf_op jit(solution)/shard_map/all_to_all | solution.py:82
  27.4 5.1 %all-to-all-done = s32[128,1,32]{2,1,0:T(1,128)S(1)} async-done(((s32[128,1,32]{2,1,0:T(1,128)}), s32[128,1,32]{2,1,0:T(1,128)S(1)}, u32[]{:S(2)}, u32[]{:S(2)}) %all-to-all-start) | async-done | bytes 16416 | tf_op jit(solution)/shard_map/all_to_all | solution.py:82
  32.5 4.7 all-to-all-start.2
  37.3 3.4 collective-permute-start.10
  43.5 3.2 all-to-all-done.2
  46.7 7.7 %all-to-all-start.3 = ((s32[128,1,32]{2,1,0:T(1,128)}), s32[128,1,32]{2,1,0:T(1,128)S(1)}, u32[]{:S(2)}, u32[]{:S(2)}) async-start(s32[128,1,32]{2,1,0:T(1,128)} %compare_convert_fusion), calls=%async_computation.3 | async-start | bytes 131072 | tf_op jit(solution)/shard_map/all_to_all | solution.py:84
  56.7 7.2 %all-to-all-done.3 = s32[128,1,32]{2,1,0:T(1,128)S(1)} async-done(((s32[128,1,32]{2,1,0:T(1,128)}), s32[128,1,32]{2,1,0:T(1,128)S(1)}, u32[]{:S(2)}, u32[]{:S(2)}) %all-to-all-start.3) | async-done | bytes 16416 | tf_op jit(solution)/shard_map/all_to_all | solution.py:84
  64.0 5.2 %all-to-all-start.1 = ((bf16[128,32,128]{2,1,0:T(8,128)(2,1)}), bf16[128,32,128]{2,1,0:T(8,128)(2,1)}, u32[]{:S(2)}, u32[]{:S(2)}) async-start(bf16[128,32,128]{2,1,0:T(8,128)(2,1)} %bitcast.1), calls=%async_computation.1 | async-start | bytes 2097152 | tf_op jit(solution)/shard_map/all_to_all | solution.py:81
  69.6 25.7 %scatter_custom_fusion.1 = f32[2048,256]{1,0:T(8,128)S(1)} fusion(s32[4096]{0:T(1024)} %copy-done.31, f32[4096]{0:T(1024)S(1)} %convert_element_type.81, f32[256]{0:T(256)} %param.12, f32[4096]{0:T(1024)S(1)} %fusion.99, f32[]{:T(128)} %constant.58.clone.1), kind=kCustom, calls=%fused_computation.8 | custom fusion | flops 3145728 | bytes 2131456 | tf_op jit(solution)/shard_map/scatter-add | solution.py:97
  96.7 3.7 convolution_multiply_fusion
  100.4 24.5 %scatter_custom_fusion = f32[2048,256]{1,0:T(8,128)} fusion(s32[4096]{0:T(1024)} %copy-done.31, f32[4096,256]{1,0:T(8,128)} %convolution_multiply_fusion, f32[]{:T(128)} %constant.48.clone.1), kind=kCustom, calls=%fused_computation.133 | custom fusion | flops 1048576 | bytes 2097664 | tf_op jit(solution)/shard_map/scatter-add | solution.py:96
  124.8 2.9 divide_convert_fusion
  127.7 2.6 copy.73
  147.3 3.5 collective-permute-start.2
  152.2 4.4 convolution_select_fusion.1
  158.8 3.3 copy.125
  162.8 2.5 maximum_bitcast_fusion
  165.3 2.8 copy.127
  169.4 3.2 reshape.209
  174.8 3.0 convolution_select_fusion.3
  180.1 3.1 copy.123
  183.2 3.8 fusion.14
  192.5 5.4 %collective-permute-start.5 = (bf16[16,1,256]{2,0,1:T(8,128)(2,1)S(1)}, bf16[16,1,256]{2,0,1:T(8,128)(2,1)S(1)}, u32[]{:S(2)}, u32[]{:S(2)}) collective-permute-start(bf16[16,1,256]{2,0,1:T(8,128)(2,1)S(1)} %copy.75), channel_id=1, source_target_pairs={{1,0},{2,1},{3,2},{4,3},{5,4},{6,5},{7,6},{8,7},{9,8},{10,9},{11,1... | collective-permute-start | bytes 24584 | tf_op jit(solution)/shard_map/ppermute | solution.py:21
  202.8 3.2 collective-permute-start.13
  206.0 4.5 pad_maximum_fusion
  221.0 4.6 collective-permute-start.14
  230.7 4.0 collective-permute-start.6
  236.1 3.6 maximum_bitcast_fusion.2
  239.7 3.9 copy.129
  243.6 2.5 pad.6.clone
  246.1 3.2 reshape.230
  251.5 3.0 convolution_select_fusion
  256.8 3.0 copy.126
  259.8 4.3 fusion.15
  264.1 2.9 copy.98
  267.1 2.5 bitcast_divide_fusion
  269.6 16.1 %gather_fusion = f32[4096,256]{1,0:T(8,128)} fusion(f32[2048,256]{1,0:T(8,128)S(1)} %bitcast_divide_fusion, s32[4096]{0:T(1024)S(1)} %copy-done.30), kind=kCustom, calls=%fused_computation | custom fusion | bytes 8404992 | tf_op jit(solution)/shard_map/jit(_take)/gather | solution.py:118
  285.8 5.7 %multiply_convert_fusion = bf16[4096,256]{1,0:T(8,128)(2,1)S(1)} fusion(f32[4096,256]{1,0:T(8,128)} %gather_fusion, f32[4096]{0:T(1024)S(1)} %copy-done.27, f32[256]{0:T(256)S(1)} %copy-done.34, f32[4096]{0:T(1024)S(1)} %copy-done.29, pred[4096]{0:T(1024)(128)(4,1)S(1)} %copy-done.32), kind=kLoop, calls=%fused_computation.6 | loop fusion | flops 5242880 | bytes 6329344 | tf_op jit(solution)/shard_map/convert_element_type | solution.py:118
  291.5 2.8 convolution_bitcast_fusion.18
  294.3 3.1 pad_maximum_fusion.1
  306.4 15.5 %all-to-all-start.4 = ((bf16[128,32,128]{2,1,0:T(8,128)(2,1)}), bf16[128,32,128]{2,1,0:T(8,128)(2,1)}, u32[]{:S(2)}, u32[]{:S(2)}) async-start(bf16[128,32,128]{2,1,0:T(8,128)(2,1)} %bitcast.195), calls=%async_computation.4 | async-start | bytes 2097152 | tf_op jit(solution)/shard_map/all_to_all | solution.py:126
  321.9 2.5 maximum_bitcast_fusion.1
  324.4 2.8 copy.128
  329.5 3.0 convolution_select_fusion.2
  338.1 2.3 copy.112
  342.6 132.4 %all-reduce.3.cloned.1.call-done = (f32[1,3,3,256,256]{4,3,2,1,0:T(8,128)}, f32[1,3,3,256,256]{4,3,2,1,0:T(8,128)}, f32[128,256]{0,1:T(8,128)}) async-done(((f32[1,3,3,256,256]{4,3,2,1,0:T(8,128)}, f32[1,3,3,256,256]{4,3,2,1,0:T(8,128)}, f32[128,256]{0,1:T(8,128)}), (f32[1,3,3,256,256]{4,3,2,1,0:T(8,128)}, f32[1,3,3,256,256]{4,3,2,1,0:T(8,128)}, f32[128,256]{0,1:T(8,128)})) %all-reduce.3.cloned.1.call-update) | async-done | bytes 4849680 | tf_op jit(solution)/shard_map/psum | solution.py:125
  476.7 5.0 %maximum_multiply_fusion = f32[2,3,3,256,256]{4,3,2,1,0:T(8,128)} fusion(f32[1,3,3,256,256]{4,3,2,1,0:T(8,128)} %get-tuple-element.16, f32[1,3,3,256,256]{4,3,2,1,0:T(8,128)} %get-tuple-element.17), kind=kLoop, calls=%fused_computation.5 | loop fusion | flops 2359296 | bytes 9437184 | tf_op jit(solution)/shard_map/mul | solution.py:135
  (191 shorter events, 94.8 us)
Async XLA Ops:
  7.2 89.5 %copy-start = (bf16[128,256]{1,0:T(8,128)(2,1)S(1)}, bf16[128,256]{1,0:T(8,128)(2,1)}, u32[]{:S(2)}) copy-start(bf16[128,256]{1,0:T(8,128)(2,1)} %param.13) | copy-start | bytes 196612
  7.2 30.0 %copy-start.1 = (bf16[16,128,256]{2,1,0:T(8,128)(2,1)S(1)}, bf16[16,128,256]{2,1,0:T(8,128)(2,1)}, u32[]{:S(2)}) copy-start(bf16[16,128,256]{2,1,0:T(8,128)(2,1)} %param.15) | copy-start | bytes 3145732
  7.2 19.5 %copy-start.33 = (s32[4096]{0:T(1024)S(1)}, s32[4096]{0:T(1024)}, u32[]{:S(2)}) copy-start(s32[4096]{0:T(1024)} %param.10) | copy-start | bytes 49156
  8.2 29.0 %collective-permute-start.8 = (bf16[16,1,256]{2,1,0:T(2,128)(2,1)S(1)}, bf16[16,1,256]{2,1,0:T(2,128)(2,1)S(1)}, u32[]{:S(2)}, u32[]{:S(2)}) collective-permute-start(bf16[16,1,256]{2,1,0:T(2,128)(2,1)S(1)} %get-tuple-element.39), channel_id=1, source_target_pairs={{0,1},{1,2},{2,3},{3,4},{4,5},{5,6},{6,7},{7,8},{8,9},{9,10},{10,1... | collective-permute-start | bytes 24584 | tf_op jit(solution)/shard_map/ppermute | solution.py:18
  11.0 26.2 %collective-permute-start.9 = (bf16[16,1,256]{2,1,0:T(2,128)(2,1)S(1)}, bf16[16,1,256]{2,1,0:T(2,128)(2,1)S(1)}, u32[]{:S(2)}, u32[]{:S(2)}) collective-permute-start(bf16[16,1,256]{2,1,0:T(2,128)(2,1)S(1)} %get-tuple-element.40), channel_id=1, source_target_pairs={{1,0},{2,1},{3,2},{4,3},{5,4},{6,5},{7,6},{8,7},{9,8},{10,9},{11,1... | collective-permute-start | bytes 24584 | tf_op jit(solution)/shard_map/ppermute | solution.py:21
  12.4 20.1 %all-to-all-start = ((s32[128,1,32]{2,1,0:T(1,128)}), s32[128,1,32]{2,1,0:T(1,128)S(1)}, u32[]{:S(2)}, u32[]{:S(2)}) async-start(s32[128,1,32]{2,1,0:T(1,128)} %bitcast), calls=%async_computation | async-start | bytes 131072 | tf_op jit(solution)/shard_map/all_to_all | solution.py:82
  32.5 14.2 %all-to-all-start.2 = ((s32[128,1,32]{2,1,0:T(1,128)}), s32[128,1,32]{2,1,0:T(1,128)S(1)}, u32[]{:S(2)}, u32[]{:S(2)}) async-start(s32[128,1,32]{2,1,0:T(1,128)} %bitcast.3), calls=%async_computation.2 | async-start | bytes 131072 | tf_op jit(solution)/shard_map/all_to_all | solution.py:83
  37.3 101.6 %collective-permute-start.10 = (bf16[1,130,256]{2,1,0:T(8,128)(2,1)S(1)}, bf16[1,130,256]{2,1,0:T(8,128)(2,1)S(1)}, u32[]{:S(2)}, u32[]{:S(2)}) collective-permute-start(bf16[1,130,256]{2,1,0:T(8,128)(2,1)S(1)} %get-tuple-element.31), channel_id=1, source_target_pairs={{0,32},{32,64},{64,96},{1,33},{33,65},{65,97},{2,34},{34,66},{66,9... | collective-permute-start | bytes 199688 | tf_op jit(solution)/shard_map/ppermute | solution.py:18
  40.7 98.1 %collective-permute-start.11 = (bf16[1,130,256]{2,1,0:T(8,128)(2,1)S(1)}, bf16[1,130,256]{2,1,0:T(8,128)(2,1)S(1)}, u32[]{:S(2)}, u32[]{:S(2)}) collective-permute-start(bf16[1,130,256]{2,1,0:T(8,128)(2,1)S(1)} %get-tuple-element.32), channel_id=1, source_target_pairs={{32,0},{64,32},{96,64},{33,1},{65,33},{97,65},{34,2},{66,34},{98,6... | collective-permute-start | bytes 199688 | tf_op jit(solution)/shard_map/ppermute | solution.py:21
  43.5 26.0 %copy-start.31 = (s32[4096]{0:T(1024)}, s32[4096]{0:T(1024)S(1)}, u32[]{:S(2)}) copy-start(s32[4096]{0:T(1024)S(1)} %reshape.274) | copy-start | bytes 49156
  46.7 17.3 %all-to-all-start.3 = ((s32[128,1,32]{2,1,0:T(1,128)}), s32[128,1,32]{2,1,0:T(1,128)S(1)}, u32[]{:S(2)}, u32[]{:S(2)}) async-start(s32[128,1,32]{2,1,0:T(1,128)} %compare_convert_fusion), calls=%async_computation.3 | async-start | bytes 131072 | tf_op jit(solution)/shard_map/all_to_all | solution.py:84
  55.4 41.2 %copy-start.28 = (f32[4096]{0:T(1024)}, f32[4096]{0:T(1024)S(1)}, u32[]{:S(2)}) copy-start(f32[4096]{0:T(1024)S(1)} %fusion.99) | copy-start | bytes 49156
  64.0 32.7 %all-to-all-start.1 = ((bf16[128,32,128]{2,1,0:T(8,128)(2,1)}), bf16[128,32,128]{2,1,0:T(8,128)(2,1)}, u32[]{:S(2)}, u32[]{:S(2)}) async-start(bf16[128,32,128]{2,1,0:T(8,128)(2,1)} %bitcast.1), calls=%async_computation.1 | async-start | bytes 2097152 | tf_op jit(solution)/shard_map/all_to_all | solution.py:81
  69.2 405.8 %all-reduce.3.cloned.1.call-start = ((), (), s32[]{:S(2)}) async-start(), calls=%async_computation.5 | async-start | bytes 9699328 | tf_op jit(solution)/shard_map/psum | solution.py:125
  69.6 30.8 %copy-start.26 = (f32[4096]{0:T(1024)}, f32[4096]{0:T(1024)S(1)}, u32[]{:S(2)}) copy-start(f32[4096]{0:T(1024)S(1)} %convert_element_type.81) | copy-start | bytes 49156
  95.3 29.6 %copy-start.12 = (f32[2048,256]{1,0:T(8,128)}, f32[2048,256]{1,0:T(8,128)S(1)}, u32[]{:S(2)}) copy-start(f32[2048,256]{1,0:T(8,128)S(1)} %scatter_custom_fusion.1) | copy-start | bytes 6291460
  137.1 8.1 %collective-permute-start.1 = (bf16[16,1,256]{2,0,1:T(8,128)(2,1)}, bf16[16,1,256]{2,0,1:T(8,128)(2,1)}, u32[]{:S(2)}, u32[]{:S(2)}) collective-permute-start(bf16[16,1,256]{2,0,1:T(8,128)(2,1)} %copy.65), channel_id=1, source_target_pairs={{1,0},{2,1},{3,2},{4,3},{5,4},{6,5},{7,6},{8,7},{9,8},{10,9},{11,1... | collective-permute-start | bytes 24584 | tf_op jit(solution)/shard_map/ppermute | solution.py:21
  138.4 5.5 %collective-permute-start = (bf16[16,1,256]{2,0,1:T(8,128)(2,1)}, bf16[16,1,256]{2,0,1:T(8,128)(2,1)}, u32[]{:S(2)}, u32[]{:S(2)}) collective-permute-start(bf16[16,1,256]{2,0,1:T(8,128)(2,1)} %copy.64), channel_id=1, source_target_pairs={{0,1},{1,2},{2,3},{3,4},{4,5},{5,6},{6,7},{7,8},{8,9},{9,10},{10,1... | collective-permute-start | bytes 24584 | tf_op jit(solution)/shard_map/ppermute | solution.py:18
  145.1 17.0 %copy-start.8 = (bf16[16,1,256]{1,2,0:T(8,128)(2,1)}, bf16[16,1,256]{1,2,0:T(8,128)(2,1)S(1)}, u32[]{:S(2)}) copy-start(bf16[16,1,256]{1,2,0:T(8,128)(2,1)S(1)} %copy.66) | copy-start | bytes 24580
  145.1 7.0 %copy-start.38 = (pred[8,17]{0,1:T(8,128)(4,1)S(1)}, pred[8,17]{0,1:T(8,128)(4,1)}, u32[]{:S(2)}) copy-start(pred[8,17]{0,1:T(8,128)(4,1)} %constant.80) | copy-start | bytes 412
  146.4 15.8 %copy-start.10 = (bf16[16,1,256]{1,2,0:T(8,128)(2,1)}, bf16[16,1,256]{1,2,0:T(8,128)(2,1)S(1)}, u32[]{:S(2)}) copy-start(bf16[16,1,256]{1,2,0:T(8,128)(2,1)S(1)} %copy.67) | copy-start | bytes 24580
  146.4 5.8 %copy-start.23 = (bf16[18,1,8,17,256]{4,2,3,0,1:T(8,128)(2,1)S(1)}, bf16[18,1,8,17,256]{4,2,3,0,1:T(8,128)(2,1)}, u32[]{:S(2)}) copy-start(bf16[18,1,8,17,256]{4,2,3,0,1:T(8,128)(2,1)} %copy-done.22) | copy-start | bytes 3760132
  147.3 14.9 %collective-permute-start.2 = (bf16[1,130,256]{1,2,0:T(8,128)(2,1)}, bf16[1,130,256]{1,2,0:T(8,128)(2,1)S(1)}, u32[]{:S(2)}, u32[]{:S(2)}) collective-permute-start(bf16[1,130,256]{1,2,0:T(8,128)(2,1)} %get-tuple-element.29), channel_id=1, source_target_pairs={{0,32},{32,64},{64,96},{1,33},{33,65},{65,97},{2,34},{34,66},{66,9... | collective-permute-start | bytes 199688 | tf_op jit(solution)/shard_map/ppermute | solution.py:18
  150.8 11.3 %collective-permute-start.3 = (bf16[1,130,256]{1,2,0:T(8,128)(2,1)}, bf16[1,130,256]{1,2,0:T(8,128)(2,1)S(1)}, u32[]{:S(2)}, u32[]{:S(2)}) collective-permute-start(bf16[1,130,256]{1,2,0:T(8,128)(2,1)} %get-tuple-element.30), channel_id=1, source_target_pairs={{32,0},{64,32},{96,64},{33,1},{65,33},{97,65},{34,2},{66,34},{98,6... | collective-permute-start | bytes 199688 | tf_op jit(solution)/shard_map/ppermute | solution.py:21
  180.1 3.1 copy-start.19
  192.5 34.9 %collective-permute-start.5 = (bf16[16,1,256]{2,0,1:T(8,128)(2,1)S(1)}, bf16[16,1,256]{2,0,1:T(8,128)(2,1)S(1)}, u32[]{:S(2)}, u32[]{:S(2)}) collective-permute-start(bf16[16,1,256]{2,0,1:T(8,128)(2,1)S(1)} %copy.75), channel_id=1, source_target_pairs={{1,0},{2,1},{3,2},{4,3},{5,4},{6,5},{7,6},{8,7},{9,8},{10,9},{11,1... | collective-permute-start | bytes 24584 | tf_op jit(solution)/shard_map/ppermute | solution.py:21
  197.9 29.0 %collective-permute-start.4 = (bf16[16,1,256]{2,0,1:T(8,128)(2,1)S(1)}, bf16[16,1,256]{2,0,1:T(8,128)(2,1)S(1)}, u32[]{:S(2)}, u32[]{:S(2)}) collective-permute-start(bf16[16,1,256]{2,0,1:T(8,128)(2,1)S(1)} %copy.74), channel_id=1, source_target_pairs={{0,1},{1,2},{2,3},{3,4},{4,5},{5,6},{6,7},{7,8},{8,9},{9,10},{10,1... | collective-permute-start | bytes 24584 | tf_op jit(solution)/shard_map/ppermute | solution.py:18
  197.9 8.1 %copy-start.25 = (bf16[1,130,256]{1,2,0:T(8,128)(2,1)S(1)}, bf16[1,130,256]{1,2,0:T(8,128)(2,1)}, u32[]{:S(2)}) copy-start(bf16[1,130,256]{1,2,0:T(8,128)(2,1)} %copy-done.24) | copy-start | bytes 199684
  202.8 15.0 %collective-permute-start.13 = (bf16[16,1,256]{2,0,1:T(8,128)(2,1)S(1)}, bf16[16,1,256]{2,0,1:T(8,128)(2,1)S(1)}, u32[]{:S(2)}, u32[]{:S(2)}) collective-permute-start(bf16[16,1,256]{2,0,1:T(8,128)(2,1)S(1)} %copy.89), channel_id=1, source_target_pairs={{1,0},{2,1},{3,2},{4,3},{5,4},{6,5},{7,6},{8,7},{9,8},{10,9},{11,1... | collective-permute-start | bytes 24584 | tf_op jit(solution)/shard_map/ppermute | solution.py:21
  206.0 11.3 %collective-permute-start.12 = (bf16[16,1,256]{2,0,1:T(8,128)(2,1)S(1)}, bf16[16,1,256]{2,0,1:T(8,128)(2,1)S(1)}, u32[]{:S(2)}, u32[]{:S(2)}) collective-permute-start(bf16[16,1,256]{2,0,1:T(8,128)(2,1)S(1)} %copy.88), channel_id=1, source_target_pairs={{0,1},{1,2},{2,3},{3,4},{4,5},{5,6},{6,7},{7,8},{8,9},{9,10},{10,1... | collective-permute-start | bytes 24584 | tf_op jit(solution)/shard_map/ppermute | solution.py:18
  217.8 3.2 copy-start.16
  221.0 15.0 %collective-permute-start.14 = (bf16[1,130,256]{1,2,0:T(8,128)(2,1)}, bf16[1,130,256]{1,2,0:T(8,128)(2,1)}, u32[]{:S(2)}, u32[]{:S(2)}) collective-permute-start(bf16[1,130,256]{1,2,0:T(8,128)(2,1)} %get-tuple-element.25), channel_id=1, source_target_pairs={{0,32},{32,64},{64,96},{1,33},{33,65},{65,97},{2,34},{34,66},{66,9... | collective-permute-start | bytes 199688 | tf_op jit(solution)/shard_map/ppermute | solution.py:18
  225.6 10.4 %collective-permute-start.15 = (bf16[1,130,256]{1,2,0:T(8,128)(2,1)}, bf16[1,130,256]{1,2,0:T(8,128)(2,1)}, u32[]{:S(2)}, u32[]{:S(2)}) collective-permute-start(bf16[1,130,256]{1,2,0:T(8,128)(2,1)} %get-tuple-element.26), channel_id=1, source_target_pairs={{32,0},{64,32},{96,64},{33,1},{65,33},{97,65},{34,2},{66,34},{98,6... | collective-permute-start | bytes 199688 | tf_op jit(solution)/shard_map/ppermute | solution.py:21
  227.4 3.3 copy-start.3
  228.8 7.2 %copy-start.17 = (bf16[16,1,256]{1,2,0:T(8,128)(2,1)S(1)}, bf16[16,1,256]{1,2,0:T(8,128)(2,1)}, u32[]{:S(2)}) copy-start(bf16[16,1,256]{1,2,0:T(8,128)(2,1)} %copy-done.16) | copy-start | bytes 24580
  228.8 7.2 %copy-start.18 = (bf16[16,1,256]{1,2,0:T(8,128)(2,1)S(1)}, bf16[16,1,256]{1,2,0:T(8,128)(2,1)}, u32[]{:S(2)}) copy-start(bf16[16,1,256]{1,2,0:T(8,128)(2,1)} %copy.91) | copy-start | bytes 24580
  230.7 63.5 %collective-permute-start.6 = (bf16[1,130,256]{1,2,0:T(8,128)(2,1)}, bf16[1,130,256]{1,2,0:T(8,128)(2,1)S(1)}, u32[]{:S(2)}, u32[]{:S(2)}) collective-permute-start(bf16[1,130,256]{1,2,0:T(8,128)(2,1)} %get-tuple-element.27), channel_id=1, source_target_pairs={{0,32},{32,64},{64,96},{1,33},{33,65},{65,97},{2,34},{34,66},{66,9... | collective-permute-start | bytes 199688 | tf_op jit(solution)/shard_map/ppermute | solution.py:18
  234.7 59.5 %collective-permute-start.7 = (bf16[1,130,256]{1,2,0:T(8,128)(2,1)}, bf16[1,130,256]{1,2,0:T(8,128)(2,1)S(1)}, u32[]{:S(2)}, u32[]{:S(2)}) collective-permute-start(bf16[1,130,256]{1,2,0:T(8,128)(2,1)} %get-tuple-element.28), channel_id=1, source_target_pairs={{32,0},{64,32},{96,64},{33,1},{65,33},{97,65},{34,2},{66,34},{98,6... | collective-permute-start | bytes 199688 | tf_op jit(solution)/shard_map/ppermute | solution.py:21
  269.6 16.2 %copy-start.27 = (f32[4096]{0:T(1024)S(1)}, f32[4096]{0:T(1024)}, u32[]{:S(2)}) copy-start(f32[4096]{0:T(1024)} %copy-done.26) | copy-start | bytes 49156
  269.6 16.2 %copy-start.29 = (f32[4096]{0:T(1024)S(1)}, f32[4096]{0:T(1024)}, u32[]{:S(2)}) copy-start(f32[4096]{0:T(1024)} %copy-done.28) | copy-start | bytes 49156
  269.6 16.2 %copy-start.32 = (pred[4096]{0:T(1024)(128)(4,1)S(1)}, pred[4096]{0:T(1024)(128)(4,1)}, u32[]{:S(2)}) copy-start(pred[4096]{0:T(1024)(128)(4,1)} %compare_and_fusion) | copy-start | bytes 12292
  269.6 16.2 %copy-start.34 = (f32[256]{0:T(256)S(1)}, f32[256]{0:T(256)}, u32[]{:S(2)}) copy-start(f32[256]{0:T(256)} %param.12) | copy-start | bytes 3076
  291.5 2.8 copy-start.4
  291.5 2.8 copy-start.6
  294.2 3.2 copy-start.2
  306.4 15.5 %copy-start.5 = (bf16[16,1,256]{1,2,0:T(8,128)(2,1)S(1)}, bf16[16,1,256]{1,2,0:T(8,128)(2,1)}, u32[]{:S(2)}) copy-start(bf16[16,1,256]{1,2,0:T(8,128)(2,1)} %copy-done.3) | copy-start | bytes 24580
  306.4 15.5 %copy-start.7 = (bf16[16,1,256]{1,2,0:T(8,128)(2,1)S(1)}, bf16[16,1,256]{1,2,0:T(8,128)(2,1)}, u32[]{:S(2)}) copy-start(bf16[16,1,256]{1,2,0:T(8,128)(2,1)} %copy.77) | copy-start | bytes 24580
  306.4 36.2 %all-to-all-start.4 = ((bf16[128,32,128]{2,1,0:T(8,128)(2,1)}), bf16[128,32,128]{2,1,0:T(8,128)(2,1)}, u32[]{:S(2)}, u32[]{:S(2)}) async-start(bf16[128,32,128]{2,1,0:T(8,128)(2,1)} %bitcast.195), calls=%async_computation.4 | async-start | bytes 2097152 | tf_op jit(solution)/shard_map/all_to_all | solution.py:126
  (13 other events, 21.3 us)
Sparse Core Ops, SparseCore 0:
  304.9 170.0 all-reduce.2
where the time goes:
time: 501 us; the launch traced here: 491 us
  waiting for transfers between devices  150 us (30%)
  local copies, waits for them, and re-layouts  110 us (22%)
  other arithmetic  106 us (21%)
  starting transfers between devices  77.5 us (15%)
  matrix products  31.9 us (6%)
  between operations  15.5 us (3%)
    psum x1, waiting for transfers between devices, on_device(): lax.psum((outer, inner, embed_sum), ('lat', 'lon'))  132 us
    unnamed x89, local copies, waits for them, and re-layouts  35.2 us
    scatter-add x1, other arithmetic, on_device(): density = jax.ops.segment_sum(weight, recv_cells, num_segments=tile_cells)  25.7 us
    scatter-add x1, other arithmetic, on_device(): jax.ops.segment_sum(embedding * weight, recv_cells, num_segments=tile_cells)  24.5 us
    conv_general_dilated x20, local copies, waits for them, and re-layouts, apply_conv(): lax.conv_general_dilated(padded[None], kernel, (1, 1), 'VALID', dimension...  24.1 us
    ppermute x8, starting transfers between devices, padded_2(): lax.ppermute(lax.slice_in_dim(block, block.shape[dim] - width, None, axis...  18.8 us
    gather x1, local copies, waits for them, and re-layouts, on_device(): jnp.take(grad_placed, recv_cells, axis=0)  16.1 us
    all_to_all x1, starting transfers between devices, on_device(): lax.all_to_all(grad_vals.reshape(devices, slot_cap, val_width), ('lat', '...  15.5 us
  transfers between devices with their start and end apart: 22, of which 5 were waited for; matrix products, arithmetic and copies ran while one was open for 39% of the time, Pallas kernels for 0%

commit v1 on v0

v1 whole, which is shorter than its diff:
```python
import jax
import jax.numpy as jnp
from jax import lax
from jax.experimental import pallas as pl
from jax.experimental.pallas import tpu as pltpu
from jax.sharding import PartitionSpec as P

F32 = jnp.float32
BF16 = jnp.bfloat16
N_LAT, N_LON = 4, 32
DEVICES = N_LAT * N_LON
CAP, VALS, CH = 32, 128, 256
ROWS, COLS = 16, 128
CELLS = ROWS * COLS
OBS = DEVICES * CAP
GROUP = 32 * CAP
PART, HALF, QUARTER, SHARD = 1536, 768, 192, 48
NT = (((1,), (1,)), ((), ()))
TN = (((0,), (0,)), ((), ()))


def dot(a, b):
    return jnp.dot(a, b, preferred_element_type=F32)


def iota(shape, axis):
    return lax.broadcasted_iota(jnp.int32, shape, axis)


def sigmoid(x):
    return 1.0 / (1.0 + jnp.exp(-x))


def remote(src, dst, send, recv, lat, lon):
    return pltpu.make_async_remote_copy(
        src_ref=src,
        dst_ref=dst,
        send_sem=send,
        recv_sem=recv,
        device_id=(lat, lon),
        device_id_type=pl.DeviceIdType.MESH,
    )


def await_bytes(ref, sem):
    pltpu.make_async_copy(ref, ref, sem).wait()


def loop(low, high, body):
    def step(i, carry):
        body(i)
        return carry

    lax.fori_loop(low, high, step, 0)


def aligned(start, size, unit):
    return pl.ds(pl.multiple_of(start, unit), size)


def kernel(
    obs_in, meta_in, sharp, embed_w, conv_in, cot_in,
    enc_out, vg_out, grads_out, embed_out,
    vals, queue, relay, meta_z, meta_x, meta, tmeta, colb, rowb, weight, ew, rk, colhot, rowl, placed, counts, inv,
    cot, conv_w, conv_t, embed_t, back, base, act_zero, mid, act_one, gmid, gp, act_t, zero_t,
    x3_act, x3_cot, x3_mid, hrow, hcol, strip, stripf,
    vg, grads, total, p0, s1, p1, s2, p2, s3, p3, esum, pe, qe, etotal, enc,
    local_sem, pair_send, pair_recv, a2a_send, a2a_recv, meta_send, meta_recv, vg_send, vg_recv,
    halo_send, halo_recv, ar_send, ar_recv, em_send, em_recv,
):
    lat = lax.axis_index("lat")
    lon = lax.axis_index("lon")
    me = lat * N_LON + lon
    xi, yi, ci = lax.div(lon, 8), lax.rem(lax.div(lon, 2), 4), lax.rem(lon, 2)

    chip = lat * 16 + xi * 4 + yi
    yc = lax.rem(lon, 8)
    other_core = lon + 1 - 2 * ci

    def offset(j):
        g, dx, dy = lax.div(j, 16), lax.rem(lax.div(j, 4), 4), lax.rem(j, 4)
        return dx, dy, lax.rem(g + 8 - dx - dy, 4)

    cot_copy = pltpu.make_async_copy(cot_in, cot, local_sem.at[0])
    cot_copy.start()
    pair_own = pltpu.make_async_copy(obs_in.at[:, ci], queue.at[:, ci], local_sem.at[4])
    pair_own.start()
    pair_other = remote(
        obs_in.at[:, 1 - ci], queue.at[:, ci], pair_send.at[0], pair_recv.at[0], lat, other_core
    )
    pair_other.start()

    def meta_copies(stage):
        copies = []
        for d in range(1, 8 if stage == 2 else 4):
            if stage == 0:
                c = lax.rem(lat + d, 4)
                src, dst, target = meta_in.at[c], meta_z.at[lat], (c, lon)
            elif stage == 1:
                c = lax.rem(xi + d, 4)
                src, dst, target = meta_z.at[:, c], meta_x.at[xi], (lat, c * 8 + yc)
            else:
                c = lax.rem(yc + d, 8)
                src, dst, target = meta_x.at[:, :, c], meta.at[yc], (lat, xi * 8 + c)
            copies.append(remote(src, dst, meta_send.at[stage], meta_recv.at[stage], *target))
        own = (
            (meta_in.at[lat], meta_z.at[lat]),
            (meta_z.at[:, xi], meta_x.at[xi]),
            (meta_x.at[:, :, yc], meta.at[yc]),
        )[stage]
        copies.append(pltpu.make_async_copy(*own, meta_recv.at[stage]))
        return copies

    def meta_start(stage):
        for copy in meta_copies(stage):
            copy.start()

    def meta_wait(stage):
        await_bytes((meta_z, meta_x, meta)[stage], meta_recv.at[stage])

    def meta_sent(stage):
        await_bytes((meta_z, meta_x, meta)[stage].at[pl.ds(0, (3, 3, 7)[stage])], meta_send.at[stage])

    meta_start(0)
    conv_copy = pltpu.make_async_copy(conv_in, conv_w, local_sem.at[1])
    conv_copy.start()

    def send_slot(j):
        dx, dy, dz = offset(j)
        tx, ty, tz = lax.rem(xi + dx, 4), lax.rem(yi + dy, 4), lax.rem(lat + dz, 4)
        g = lax.div(j, 16)
        remote(
            queue.at[tz * 16 + tx * 4 + ty], vals.at[j], a2a_send.at[g], a2a_recv.at[g],
            tz, tx * 8 + ty * 2 + ci,
        ).start()

    north, south = lax.rem(lat + 3, N_LAT), lax.rem(lat + 1, N_LAT)
    west, east = lax.rem(lon + N_LON - 1, N_LON), lax.rem(lon + 1, N_LON)

    def halo_copies(src, k):
        pieces = [
            (src.at[ROWS - 1], hrow.at[k, 0], south, lon),
            (src.at[0], hrow.at[k, 1], north, lon),
        ]
        for side, column, target in ((0, 1, east), (1, 0, west)):
            for turn, tlat in enumerate((lat, south, north)):
                pieces.append((strip.at[k, column], hcol.at[k, side, turn], tlat, target))
        return [
            remote(s, d, halo_send.at[k, i], halo_recv.at[k, i], a, b)
            for i, (s, d, a, b) in enumerate(pieces)
        ]

    def halo_start(src, k):
        for r in range(ROWS):
            stripf[0, r : r + 1, :] = src[r, 0:16, :].astype(F32)[0:1, :]
            stripf[1, r : r + 1, :] = src[r, COLS - 16 : COLS, :].astype(F32)[15:16, :]
        strip[k, 0] = stripf[0].astype(BF16)
        strip[k, 1] = stripf[1].astype(BF16)
        for copy in halo_copies(src, k):
            copy.start()

    def widen(src, x3):
        def body(r):
            row = src[r].astype(F32)
            x3[r + 1, :, 0:CH] = pltpu.roll(row, 1, 0).astype(BF16)
            x3[r + 1, :, CH : 2 * CH] = src[r]
            x3[r + 1, :, 2 * CH : 3 * CH] = pltpu.roll(row, COLS - 1, 0).astype(BF16)

        loop(0, ROWS, body)

    def halo_finish(src, k, x3):
        for copy in halo_copies(src, k):
            copy.wait()
        first = iota((16, CH), 0) == 0
        last = iota((16, CH), 0) == 15
        left = hcol[k, 0, 0].astype(F32)
        right = hcol[k, 1, 0].astype(F32)
        for r in range(ROWS):
            low = x3[r + 1, 0:16, 0:CH].astype(F32)
            x3[r + 1, 0:16, 0:CH] = jnp.where(first, left[r : r + 1, :], low).astype(BF16)
            high = x3[r + 1, COLS - 16 : COLS, 2 * CH : 3 * CH].astype(F32)
            x3[r + 1, COLS - 16 : COLS, 2 * CH : 3 * CH] = jnp.where(
                last, right[r : r + 1, :], high
            ).astype(BF16)
        spot = iota((COLS, CH), 0)
        for side, r, turn, pick, valid in (
            (0, 0, 1, ROWS - 1, lat > 0),
            (1, ROWS + 1, 2, 0, lat < N_LAT - 1),
        ):
            keep = jnp.where(valid, 1.0, 0.0).astype(F32)
            row = hrow[k, side].astype(F32) * keep
            lcorner = hcol[k, 0, turn].astype(F32)[pick : pick + 1, :] * keep
            rcorner = hcol[k, 1, turn].astype(F32)[pick : pick + 1, :] * keep
            x3[r, :, 0:CH] = jnp.where(spot == 0, lcorner, pltpu.roll(row, 1, 0)).astype(BF16)
            x3[r, :, CH : 2 * CH] = row.astype(BF16)
            x3[r, :, 2 * CH : 3 * CH] = jnp.where(
                spot == COLS - 1, rcorner, pltpu.roll(row, COLS - 1, 0)
            ).astype(BF16)

    def conv(x3, w, k, finish, low=0, high=4):
        def body(b):
            acc = jnp.zeros((4 * COLS, CH), F32)
            for p in range(3):
                acc += dot(x3[pl.ds(4 * b + p, 4)].reshape(4 * COLS, 3 * CH), w[k, p])
            finish(pl.ds(4 * b, 4), acc)

        loop(low, high, body)

    def tile4(x):
        return x.reshape(4 * COLS, CH)

    def grid4(x):
        return x.reshape(4, COLS, CH)

    def turn_weights(k):
        for p in range(3):
            for q in range(3):
                block = conv_w[k, 2 - p, (2 - q) * CH : (3 - q) * CH, :]
                conv_t[k, p, q * CH : (q + 1) * CH, :] = block.T

    def turn_act(act, act_t):
        for r in range(ROWS):
            act_t[:, r * COLS : (r + 1) * COLS] = act[r].T

    cot_copy.wait()
    halo_start(cot, 0)
    meta_wait(0)
    meta_start(1)
    pair_own.wait()
    pair_other.wait()
    pltpu.make_async_copy(queue.at[chip], vals.at[0], a2a_recv.at[0]).start()
    loop(1, 64, send_slot)
    widen(cot, x3_cot)
    meta_wait(1)
    meta_start(2)
    conv_copy.wait()
    turn_weights(1)
    embed_t[...] = embed_w[...].T
    halo_finish(cot, 0, x3_cot)

    def keep_back(rows, acc):
        back[rows] = grid4(acc)

    conv(x3_cot, conv_t, 1, keep_back)
    meta_wait(2)

    placed[...] = jnp.zeros_like(placed)
    counts[...] = jnp.zeros_like(counts)
    slot_mask = jnp.where(
        lax.rem(iota((CAP, 128), 1), 32) == iota((CAP, 128), 0), 1.0, 0.0
    ).astype(F32)
    spread = jnp.where(
        lax.div(iota((128, 512), 0), 32) == lax.div(iota((128, 512), 1), 128), 1.0, 0.0
    ).astype(BF16)
    lane, line = iota((COLS + 16, 128), 1), iota((COLS + 16, 128), 0)
    pick = jnp.where(lax.div(lane, 32) == jnp.where(line < COLS, 0, 3), 1.0, 0.0).astype(BF16)
    decay = sharp[...] * (-1.0 / 256.0)

    for g in range(4):
        def stretch(s, g=g):
            dx, dy, dz = offset(g * 16 + lax.div(s, 2))
            sx, sy, sz = lax.rem(xi + 4 - dx, 4), lax.rem(yi + 4 - dy, 4), lax.rem(lat + 4 - dz, 4)
            source = meta[sy * 2 + lax.rem(s, 2), sx, sz]
            line = jnp.broadcast_to(source, (CAP, 128)) * slot_mask
            tmeta[aligned(s * CAP, CAP, CAP), :] = line.astype(BF16)

        loop(0, 32, stretch)
        await_bytes(vals.at[pl.ds(g * 16, 16)], a2a_recv.at[g])

        def embed_block(b, g=g):
            at = aligned(b * 256, 256, 256)
            of = aligned(g * GROUP + b * 256, 256, 256)
            wide = dot(tmeta[at, :], spread)
            colb[of, :] = wide[:, 0:128].astype(BF16)
            rowb[of, :] = wide[:, 384:512].astype(BF16)
            rk_of = jnp.concatenate([wide[:, 128:256]] * 2, axis=1)
            radius = jnp.concatenate([wide[:, 256:384]] * 2, axis=1)
            rk[at, :] = jnp.where(
                rk_of == iota((256, 256), 1).astype(F32), 1.0, 0.0
            ).astype(BF16)
            w = jnp.exp(radius * decay)
            weight[of, :] = w
            ew[at, :] = (dot(vals[pl.ds(g * 16 + 4 * b, 4)].reshape(256, VALS), embed_w[...]) * w).astype(BF16)

        loop(0, 4, embed_block)
        both = lax.dot_general(pick, tmeta[...], NT, preferred_element_type=F32)
        colhot[...] = jnp.where(
            both[0:COLS] == iota((COLS, GROUP), 0).astype(F32), 1.0, 0.0
        ).astype(BF16)
        rowl[...] = both[COLS : COLS + 16]
        counts[...] += dot(colhot[...], rk[...])

        def place(pair):
            hot = colhot[...].reshape(8, 16, GROUP)
            halves = []
            for h in range(2):
                r = (2 * pair + h).astype(F32)
                mask = jnp.where(rowl[...] == r, 1.0, 0.0).astype(BF16)
                halves.append((hot * mask[None]).reshape(COLS, GROUP))
            at = aligned(pair * 256, 256, 256)
            placed[at, :] += dot(jnp.concatenate(halves, axis=0), ew[...])

        loop(0, 8, place)

    tally = counts[...].astype(BF16)
    kind = lax.rem(iota((256, CH), 0), 16)
    half_u, half_v = 2 * lax.div(kind, 4) + 1, 2 * lax.rem(kind, 4) + 1
    table = jnp.exp((half_u * half_u + half_v * half_v).astype(F32) * decay)
    table_hi = table.astype(BF16)
    table_lo = (table - table_hi.astype(F32)).astype(BF16)

    def base_row(r):
        own = lax.div(iota((256, CH), 0), 16) == r
        hi = jnp.where(own, table_hi.astype(F32), 0.0).astype(BF16)
        lo = jnp.where(own, table_lo.astype(F32), 0.0).astype(BF16)
        recip = 1.0 / (dot(tally, hi) + dot(tally, lo) + 1.0)
        inv[r] = recip
        value = (placed[aligned(r * COLS, COLS, COLS), :] * recip).astype(BF16)
        base[r] = value
        x = value.astype(F32)
        act_zero[r] = (x * sigmoid(x)).astype(BF16)

    loop(0, ROWS, base_row)
    halo_start(act_zero, 1)
    widen(act_zero, x3_act)
    turn_weights(0)
    turn_act(act_zero, zero_t)
    halo_finish(act_zero, 1, x3_act)

    def keep_mid(rows, acc):
        value = (tile4(base[rows]).astype(F32) + acc).astype(BF16)
        mid[rows] = grid4(value)
        x = value.astype(F32)
        s = sigmoid(x)
        act_one[rows] = grid4((x * s).astype(BF16))
        slope = s * (1.0 + x * (1.0 - s))
        grad = tile4(cot[rows]).astype(F32) + tile4(back[rows]) * slope
        gmid[rows] = grid4(grad.astype(BF16))

    conv(x3_act, conv_w, 0, keep_mid)
    halo_start(gmid, 2)
    halo_start(act_one, 3)

    def kernel_grad(act_t, x3, k):
        def body(p):
            block = dot(act_t[...], x3[pl.ds(2 - p, ROWS)].reshape(CELLS, 3 * CH))
            for q in range(3):
                at = aligned((k * 9 + 3 * p + q) * CH, CH, CH)
                grads[at, :] = block[:, (2 - q) * CH : (3 - q) * CH].astype(BF16)

        loop(0, 3, body)

    turn_act(act_one, act_t)
    kernel_grad(act_t, x3_cot, 1)
    widen(gmid, x3_mid)
    halo_finish(gmid, 2, x3_mid)
    kernel_grad(zero_t, x3_mid, 0)

    coords = {"x": xi, "y": yi, "z": lat}
    orders = (("x", "y", "z"), ("y", "z", "x"), ("z", "x", "y"))

    def along(axis, c):
        cx, cy, cz = [c if axis == n else coords[n] for n in ("x", "y", "z")]
        return cz, cx * 8 + cy * 2 + ci

    def turned(axis, d):
        return lax.rem(coords[axis] + d, 4)

    def part_copies(stage):
        copies = []
        for a, order in enumerate(orders):
            own = a * PART + ci * HALF
            sems = lambda d: (ar_send.at[stage, a, d], ar_recv.at[stage, a, d])
            quarter = own + coords[order[0]] * QUARTER
            shard = quarter + coords[order[1]] * SHARD
            if stage == 0:
                src = grads.at[aligned(a * PART + (1 - ci) * HALF, HALF, 16)]
                copies.append(remote(src, p0.at[a], *sems(0), lat, other_core))
            elif stage == 6:
                piece = total.at[aligned(own, HALF, 16)]
                copies.append(remote(piece, piece, *sems(0), lat, other_core))
            else:
                axis = order[{1: 0, 2: 1, 3: 2, 4: 1, 5: 0}[stage]]
                for d in (1, 3, 2):
                    c = turned(axis, d)
                    if stage == 1:
                        src, dst = s1.at[a, aligned(c * QUARTER, QUARTER, 16)], p1.at[a, d - 1]
                    elif stage == 2:
                        src, dst = s2.at[a, aligned(c * SHARD, SHARD, 16)], p2.at[a, d - 1]
                    elif stage == 3:
                        src, dst = s3.at[a], p3.at[a, coords[axis]]
                    elif stage == 4:
                        src = dst = total.at[aligned(shard, SHARD, 16)]
                    else:
                        src = dst = total.at[aligned(quarter, QUARTER, 16)]
                    copies.append(remote(src, dst, *sems(d - 1), *along(axis, c)))
        return copies

    def ar_start(stage):
        for copy in part_copies(stage):
            copy.start()

    def ar_finish(stage):
        for copy in part_copies(stage):
            copy.wait()
        for a, order in enumerate(orders):
            own = a * PART + ci * HALF
            if stage == 0:

                def body(b, a=a, own=own):
                    here = grads[aligned(own + b * QUARTER, QUARTER, 16), :].astype(F32)
                    at = aligned(b * QUARTER, QUARTER, 16)
                    s1[a, at, :] = (here + p0[a, at, :].astype(F32)).astype(BF16)

                loop(0, 4, body)
            elif stage in (1, 2):
                size = QUARTER if stage == 1 else SHARD
                src, came, dst = (s1, p1, s2) if stage == 1 else (s2, p2, s3)
                here = src[a, aligned(coords[order[stage - 1]] * size, size, 16), :].astype(F32)
                for d in range(3):
                    here += came[a, d].astype(F32)
                dst[a] = here.astype(BF16)
            elif stage == 3:
                p3[a, coords[order[2]]] = s3[a]
                whole = p3[a, 0].astype(F32)
                for d in range(1, 4):
                    whole += p3[a, d].astype(F32)
                quarter = own + coords[order[0]] * QUARTER
                at = aligned(quarter + coords[order[1]] * SHARD, SHARD, 16)
                total[at, :] = whole.astype(BF16)

    ar_start(0)

    def keep_gp(rows, acc):
        x = tile4(base[rows]).astype(F32)
        s = sigmoid(x)
        grad = tile4(gmid[rows]).astype(F32) + acc * (s * (1.0 + x * (1.0 - s)))
        gp[aligned(rows.start * COLS, 4 * COLS, 4 * COLS), :] = (
            grad * tile4(inv[rows])
        ).astype(BF16)

    conv(x3_mid, conv_t, 0, keep_gp)
    ar_finish(0)
    ar_start(1)

    esum[...] = jnp.zeros_like(esum)

    def vg_copy(j):
        dx, dy, dz = offset(j)
        sx, sy, sz = lax.rem(xi + 4 - dx, 4), lax.rem(yi + 4 - dy, 4), lax.rem(lat + 4 - dz, 4)
        return remote(vg.at[j], relay.at[chip], vg_send, vg_recv, sz, sx * 8 + sy * 2 + ci)

    def gather(b):
        at = aligned(b * 256, 256, 256)
        hot = jnp.where(
            colb[at, :].astype(F32) == iota((256, COLS), 1).astype(F32), 1.0, 0.0
        ).astype(BF16)
        row_of = rowb[at, :]
        pieces = [
            jnp.where(row_of == jnp.array(r, BF16), hot, jnp.zeros_like(hot)) for r in range(ROWS)
        ]
        found = dot(jnp.concatenate(pieces, axis=1), gp[...])
        grad = (found * weight[at, :]).astype(BF16)
        vg[pl.ds(4 * b, 4)] = dot(grad, embed_t[...]).astype(BF16).reshape(4, 2, CAP, VALS)
        own = vals[pl.ds(4 * b, 4)].reshape(256, VALS)
        esum[...] += lax.dot_general(own, grad, TN, preferred_element_type=F32)

    gather(0)
    pltpu.make_async_copy(vg.at[0], relay.at[chip], vg_recv).start()
    for j in range(1, 4):
        vg_copy(j).start()

    def gather_send(b):
        gather(b)
        for s in range(4):
            vg_copy(b * 4 + s).start()

    loop(1, 6, gather_send)
    ar_finish(1)
    ar_start(2)
    loop(6, 9, gather_send)
    ar_finish(2)
    ar_start(3)
    loop(9, 12, gather_send)
    ar_finish(3)
    ar_start(4)
    loop(12, 16, gather_send)
    ar_finish(4)
    ar_start(5)

    member = yc
    column = xi * 4 + lat

    def embed_copies(stage):
        copies = []
        for d in range(1, 16 if stage == 1 else 8):
            if stage == 1:
                c = lax.rem(column + d, 16)
                tlat, tlon = lax.rem(c, 4), lax.div(c, 4) * 8 + member
                src, dst = esum.at[aligned(member * 16, 16, 16)], qe.at[column]
            else:
                m = lax.rem(member + d, 8)
                tlat, tlon = lat, xi * 8 + m
                if stage == 0:
                    src, dst = esum.at[aligned(m * 16, 16, 16)], pe.at[d - 1]
                else:
                    src = dst = etotal.at[aligned(member * 16, 16, 16)]
            copies.append(remote(src, dst, em_send.at[stage, d - 1], em_recv.at[stage, d - 1], tlat, tlon))
        return copies

    def embed_start(stage):
        for copy in embed_copies(stage):
            copy.start()

    def embed_wait(stage):
        for copy in embed_copies(stage):
            copy.wait()

    embed_start(0)
    widen(act_one, x3_act)
    halo_finish(act_one, 3, x3_act)

    def keep_enc(rows, acc):
        enc[rows] = grid4((tile4(mid[rows]).astype(F32) + acc).astype(BF16))

    conv(x3_act, conv_w, 1, keep_enc, 0, 2)
    embed_wait(0)
    own_rows = aligned(member * 16, 16, 16)
    mine = esum[own_rows, :]
    for d in range(7):
        mine += pe[d]
    esum[own_rows, :] = mine
    embed_start(1)
    conv(x3_act, conv_w, 1, keep_enc, 2, 4)
    enc_copy = pltpu.make_async_copy(enc, enc_out, local_sem.at[2])
    enc_copy.start()
    embed_wait(1)
    qe[column] = esum[own_rows, :]
    whole = qe[0]
    for d in range(1, 16):
        whole += qe[d]
    etotal[own_rows, :] = whole
    embed_start(2)
    ar_finish(5)
    ar_start(6)
    await_bytes(relay, vg_recv)
    vg_own = pltpu.make_async_copy(relay.at[:, ci], vg_out.at[:, ci], local_sem.at[5])
    vg_own.start()
    vg_other = remote(
        relay.at[:, 1 - ci], vg_out.at[:, ci], pair_send.at[1], pair_recv.at[1], lat, other_core
    )
    vg_other.start()
    ar_finish(6)
    grads_copy = pltpu.make_async_copy(total, grads_out, local_sem.at[3])
    grads_copy.start()
    embed_wait(2)
    embed_out[...] = etotal[...] * (1.0 / 512.0)
    for g in range(4):
        await_bytes(vals.at[pl.ds(0, 15 if g == 0 else 16)], a2a_send.at[g])
    for stage in range(3):
        meta_sent(stage)
    await_bytes(vg.at[pl.ds(0, 63)], vg_send)
    vg_own.wait()
    vg_other.wait()
    enc_copy.wait()
    grads_copy.wait()


def scaled(grads_ref, out_ref):
    out_ref[...] = grads_ref[...].astype(F32) * (1.0 / 512.0)


def on_device(
    obs_values, obs_cells, obs_subcell, slot_counts, sharpness, embed_weight, conv_weight, cotangent
):
    cells = obs_cells.reshape(DEVICES, 1, CAP)
    subs = obs_subcell.reshape(DEVICES, 1, CAP)
    spread = (DEVICES, 4, CAP)
    live = lax.broadcasted_iota(jnp.int32, spread, 2) < slot_counts.reshape(DEVICES, 1, 1)
    field = lax.broadcasted_iota(jnp.int32, spread, 1)
    i, j = subs >> 3, subs & 7
    u = jnp.where(i >= 4, i - 4, 3 - i)
    v = jnp.where(j >= 4, j - 4, 3 - j)
    row = cells >> 7
    radius = (2 * u + 1) * (2 * u + 1) + (2 * v + 1) * (2 * v + 1)
    column = jnp.where(live, cells & 127, 255)
    rest = jnp.where(field == 1, row * 16 + u * 4 + v, jnp.where(field == 2, radius, row))
    meta = jnp.where(field == 0, column, rest).astype(F32)
    anywhere = pl.BlockSpec(memory_space=pl.ANY)
    vmem = pl.BlockSpec(memory_space=pltpu.VMEM)
    grid = (ROWS, COLS, CH)
    wide = (ROWS + 2, COLS, 3 * CH)
    dma = pltpu.SemaphoreType.DMA
    scratch = [
        pltpu.VMEM((64, 2, CAP, VALS), BF16),
        pltpu.VMEM((64, 2, CAP, VALS), BF16),
        pltpu.VMEM((64, 2, CAP, VALS), BF16),
        pltpu.VMEM((4, 4, 8, 1, 128), F32),
        pltpu.VMEM((4, 4, 8, 1, 128), F32),
        pltpu.VMEM((8, 4, 4, 1, 128), F32),
        pltpu.VMEM((GROUP, 128), BF16),
        pltpu.VMEM((OBS, 128), BF16),
        pltpu.VMEM((OBS, 128), BF16),
        pltpu.VMEM((OBS, CH), F32),
        pltpu.VMEM((GROUP, CH), BF16),
        pltpu.VMEM((GROUP, 256), BF16),
        pltpu.VMEM((COLS, GROUP), BF16),
        pltpu.VMEM((16, GROUP), F32),
        pltpu.VMEM((CELLS, CH), F32),
        pltpu.VMEM((COLS, 256), F32),
        pltpu.VMEM(grid, F32),
        pltpu.VMEM(grid, BF16),
        pltpu.VMEM((2, 3, 3 * CH, CH), BF16),
        pltpu.VMEM((2, 3, 3 * CH, CH), BF16),
        pltpu.VMEM((CH, VALS), BF16),
        pltpu.VMEM(grid, F32),
        pltpu.VMEM(grid, BF16),
        pltpu.VMEM(grid, BF16),
        pltpu.VMEM(grid, BF16),
        pltpu.VMEM(grid, BF16),
        pltpu.VMEM(grid, BF16),
        pltpu.VMEM((CELLS, CH), BF16),
        pltpu.VMEM((CH, CELLS), BF16),
        pltpu.VMEM((CH, CELLS), BF16),
        pltpu.VMEM(wide, BF16),
        pltpu.VMEM(wide, BF16),
        pltpu.VMEM(wide, BF16),
        pltpu.VMEM((4, 2, COLS, CH), BF16),
        pltpu.VMEM((4, 2, 3, 16, CH), BF16),
        pltpu.VMEM((4, 2, 16, CH), BF16),
        pltpu.VMEM((2, 16, CH), F32),
        pltpu.VMEM((64, 2, CAP, VALS), BF16),
        pltpu.VMEM((3 * PART, CH), BF16),
        pltpu.VMEM((3 * PART, CH), BF16),
        pltpu.VMEM((3, HALF, CH), BF16),
        pltpu.VMEM((3, HALF, CH), BF16),
        pltpu.VMEM((3, 3, QUARTER, CH), BF16),
        pltpu.VMEM((3, QUARTER, CH), BF16),
        pltpu.VMEM((3, 3, SHARD, CH), BF16),
        pltpu.VMEM((3, SHARD, CH), BF16),
        pltpu.VMEM((3, 4, SHARD, CH), BF16),
        pltpu.VMEM((VALS, CH), F32),
        pltpu.VMEM((7, 16, CH), F32),
        pltpu.VMEM((16, 16, CH), F32),
        pltpu.VMEM((VALS, CH), F32),
        pltpu.VMEM(grid, BF16),
        dma((6,)),
        dma((2,)),
        dma((2,)),
        dma((4,)),
        dma((4,)),
        dma((3,)),
        dma((3,)),
        dma,
        dma,
        dma((4, 8)),
        dma((4, 8)),
        dma((7, 3, 3)),
        dma((7, 3, 3)),
        dma((3, 15)),
        dma((3, 15)),
    ]
    encoded, value_grads, grads, embed_total = pl.pallas_call(
        kernel,
        out_shape=(
            jax.ShapeDtypeStruct(grid, BF16),
            jax.ShapeDtypeStruct((64, 2, CAP, VALS), BF16),
            jax.ShapeDtypeStruct((3 * PART, CH), BF16),
            jax.ShapeDtypeStruct((VALS, CH), F32),
        ),
        in_specs=[anywhere, anywhere, vmem, vmem, anywhere, anywhere],
        out_specs=(anywhere, anywhere, anywhere, vmem),
        scratch_shapes=scratch,
        compiler_params=pltpu.CompilerParams(
            has_side_effects=True, vmem_limit_bytes=60 * 1024 * 1024
        ),
        cost_estimate=pl.CostEstimate(
            flops=30_000_000_000, bytes_accessed=20_000_000, transcendentals=4_000_000
        ),
    )(
        obs_values.reshape(64, 2, CAP, VALS),
        meta.reshape(4, 4, 8, 1, 128),
        sharpness.reshape(1, CH),
        embed_weight,
        conv_weight.reshape(2, 3, 3 * CH, CH),
        cotangent,
    )
    conv_grads = pl.pallas_call(
        scaled,
        grid=(6,),
        out_shape=jax.ShapeDtypeStruct((3 * PART, CH), F32),
        in_specs=[pl.BlockSpec((HALF, CH), lambda i: (i, 0))],
        out_specs=pl.BlockSpec((HALF, CH), lambda i: (i, 0)),
    )(grads)
    return (
        encoded,
        value_grads.reshape(OBS, VALS),
        conv_grads.reshape(2, 3, 3, CH, CH),
        embed_total,
    )


def solution(mesh):
    placed = (
        P(("lat", "lon"), None),
        P(("lat", "lon")),
        P(("lat", "lon")),
        P(("lat", "lon"), None),
        P(),
        P(),
        P(),
        P("lat", "lon", None),
    )
    return jax.shard_map(
        on_device,
        mesh=mesh,
        in_specs=placed,
        out_specs=(P("lat", "lon", None), P(("lat", "lon"), None), P(), P()),
        check_vma=False,
    )
```

time: 501 us -> 138 us (0.28); the launches traced: 491 us -> 137 us
  waiting for transfers between devices: 150 us -> 0 us
  Pallas kernels: 0 us -> 127 us
  local copies, waits for them, and re-layouts: 110 us -> 5.63 us
  other arithmetic: 106 us -> 3.67 us
  starting transfers between devices: 77.5 us -> 0 us
  matrix products: 31.9 us -> 0 us
  between operations: 15.5 us -> 0.72 us
    psum x1 -> x0, waiting for transfers between devices: 132 us -> none  [on_device(): lax.psum((outer, inner, embed_sum), ('lat', 'lon'))]
    pallas_call x0 -> x2, Pallas kernels: none -> 127 us  [the longest x1 122 us: on_device(): pl.pallas_call(kernel, out_shape=(jax.ShapeDtypeStruct(grid, BF16), jax.S...]
    scatter-add x2 -> x0, other arithmetic: 50.2 us -> none  [the longest x1 25.7 us: on_device(): density = jax.ops.segment_sum(weight, recv_cells, num_segments=tile_cells)]
    all_to_all x5 -> x0, starting transfers between devices: 43.7 us -> none  [the longest x1 15.5 us: on_device(): lax.all_to_all(grad_vals.reshape(devices, slot_cap, val_width), ('lat', '...]
    ppermute x16 -> x0, starting transfers between devices: 33.8 us -> none  [the longest x8 18.8 us: padded_2(): lax.ppermute(lax.slice_in_dim(block, block.shape[dim] - width, None, axis...]
    unnamed x89 -> x10, local copies, waits for them, and re-layouts: 35.2 us -> 3.74 us
    conv_general_dilated x20 -> x0, local copies, waits for them, and re-layouts: 24.1 us -> none  [apply_conv(): lax.conv_general_dilated(padded[None], kernel, (1, 1), 'VALID', dimension...]
    dot_general x21 -> x0, matrix products: 18.4 us -> none  [the longest x18 10.2 us: kernel_grad(): jnp.einsum('hwc,hwo->co', window, grad, preferred_element_type=jnp.float32)]
  transfers between devices with their start and end apart: 22 -> 0, of which waited for: 5 -> 0; matrix products, arithmetic and copies ran while one was open for 39% -> 0% of each run, Pallas kernels for 0% -> 0%
where the time goes in v1:
time: 138 us; the launch traced here: 137 us
  Pallas kernels  127 us (92%)
  local copies, waits for them, and re-layouts  5.63 us (4%)
  other arithmetic  3.67 us (3%)
    pallas_call x1, Pallas kernels, on_device(): pl.pallas_call(kernel, out_shape=(jax.ShapeDtypeStruct(grid, BF16), jax.S...  122 us
    pallas_call x1, Pallas kernels, on_device(): pl.pallas_call(scaled, grid=(6,), out_shape=jax.ShapeDtypeStruct((3 * PAR...  5.33 us
    unnamed x10, local copies, waits for them, and re-layouts  3.74 us

profile of v1, /device:TPU:1, one launch (start us, length us, event | category | flops | bytes accessed | tf_op | source)
XLA Modules:
  0.0 137.2 jit_solution(10722901166806757426)
XLA Ops:
  0.6 0.5 broadcast.236
  1.1 1.3 reduce.3
  2.5 0.1 iota.38
  2.5 0.1 iota.39
  2.6 0.1 iota.45
  2.7 0.1 iota.46
  2.8 0.1 iota.49
  2.9 0.1 iota.50
  3.0 0.1 iota.42
  3.1 0.1 lt.17
  3.2 0.7 broadcast_and_fusion
  3.9 0.1 and.28
  4.0 0.7 add_multiply_fusion
  4.7 0.1 reshape.196
  4.8 0.1 shift_right_arithmetic.27
  4.9 0.1 select_n.74
  4.9 0.1 mul.62
  5.1 0.2 broadcast_in_dim.50
  5.3 0.2 broadcast_in_dim.52
  5.5 0.2 broadcast_in_dim.45
  5.8 0.2 broadcast_in_dim.48
  5.9 0.8 fusion.meta_in
  6.8 121.8 %shard_map.111 = (bf16[16,128,256]{2,1,0:T(8,128)(2,1)}, bf16[64,2,32,128]{3,2,1,0:T(8,128)(2,1)}, bf16[4608,256]{1,0:T(8,128)(2,1)}, f32[128,256]{1,0:T(8,128)}) custom-call(bf16[64,2,32,128]{3,2,1,0:T(8,128)(2,1)} %bitcast.16, f32[4,4,8,1,128]{4,3,2,1,0:T(1,128)} %fusion.meta_in, f32[1,256]{1,0:T(1,128)} %bitcast.17, bf16[128,256]{1,0:T(8,128)(2,1)} %embed_w.1, ...), custom_call_target="tpu_custom_call" | custom-call | flops 30000001024 | bytes 20000000 | tf_op jit(solution)/shard_map/pallas_call | solution.py:663
  128.6 0.0 copy-start.1
  128.6 5.3 %shard_map.112 = f32[4608,256]{1,0:T(8,128)} custom-call(bf16[4608,256]{1,0:T(8,128)(2,1)} %get-tuple-element.10.grads_ref), custom_call_target="tpu_custom_call" | custom-call | tf_op jit(solution)/shard_map/pallas_call | solution.py:688
  133.9 0.0 copy-start
  133.9 0.0 copy-start.2
  134.0 0.0 copy-done.1
  134.0 1.0 copy.19
  134.9 0.6 copy-done
  135.6 1.0 copy.20
  136.5 0.0 copy-done.2
  136.5 0.7 copy.21
  (9 shorter events, 0.2 us)
Async XLA Ops:
  128.6 5.4 %copy-start.1 = (bf16[16,128,256]{2,1,0:T(8,128)(2,1)S(1)}, bf16[16,128,256]{2,1,0:T(8,128)(2,1)}, u32[]{:S(2)}) copy-start(bf16[16,128,256]{2,1,0:T(8,128)(2,1)} %get-tuple-element.23) | copy-start | bytes 3145732
  133.9 1.6 %copy-start = (bf16[64,2,32,128]{3,2,1,0:T(8,128)(2,1)S(1)}, bf16[64,2,32,128]{3,2,1,0:T(8,128)(2,1)}, u32[]{:S(2)}) copy-start(bf16[64,2,32,128]{3,2,1,0:T(8,128)(2,1)} %get-tuple-element.9) | copy-start | bytes 3145732
  133.9 2.6 %copy-start.2 = (f32[128,256]{1,0:T(8,128)S(1)}, f32[128,256]{1,0:T(8,128)}, u32[]{:S(2)}) copy-start(f32[128,256]{1,0:T(8,128)} %get-tuple-element.26) | copy-start | bytes 393220

commit v2 on v1

--- a/solution.py
+++ b/solution.py
@@ -160,13 +160,15 @@
             copy.start()
 
     def widen(src, x3):
-        def body(r):
-            row = src[r].astype(F32)
-            x3[r + 1, :, 0:CH] = pltpu.roll(row, 1, 0).astype(BF16)
-            x3[r + 1, :, CH : 2 * CH] = src[r]
-            x3[r + 1, :, 2 * CH : 3 * CH] = pltpu.roll(row, COLS - 1, 0).astype(BF16)
-
-        loop(0, ROWS, body)
+        def body(b):
+            for i in range(4):
+                r = 4 * b + i
+                row = src[r].astype(F32)
+                x3[r + 1, :, 0:CH] = pltpu.roll(row, 1, 0).astype(BF16)
+                x3[r + 1, :, CH : 2 * CH] = src[r]
+                x3[r + 1, :, 2 * CH : 3 * CH] = pltpu.roll(row, COLS - 1, 0).astype(BF16)
+
+        loop(0, ROWS // 4, body)
 
     def halo_finish(src, k, x3):
         for copy in halo_copies(src, k):
@@ -198,13 +200,10 @@
             ).astype(BF16)
 
     def conv(x3, w, k, finish, low=0, high=4):
-        def body(b):
-            acc = jnp.zeros((4 * COLS, CH), F32)
-            for p in range(3):
-                acc += dot(x3[pl.ds(4 * b + p, 4)].reshape(4 * COLS, 3 * CH), w[k, p])
-            finish(pl.ds(4 * b, 4), acc)
-
-        loop(low, high, body)
+        taps = w[k].reshape(9 * CH, CH)
+        for b in range(low, high):
+            near = [x3[4 * b + p : 4 * b + p + 4].reshape(4 * COLS, 3 * CH) for p in range(3)]
+            finish(slice(4 * b, 4 * b + 4), dot(jnp.concatenate(near, axis=1), taps))
 
     def tile4(x):
         return x.reshape(4 * COLS, CH)
@@ -257,19 +256,21 @@
     decay = sharp[...] * (-1.0 / 256.0)
 
     for g in range(4):
-        def stretch(s, g=g):
-            dx, dy, dz = offset(g * 16 + lax.div(s, 2))
-            sx, sy, sz = lax.rem(xi + 4 - dx, 4), lax.rem(yi + 4 - dy, 4), lax.rem(lat + 4 - dz, 4)
-            source = meta[sy * 2 + lax.rem(s, 2), sx, sz]
-            line = jnp.broadcast_to(source, (CAP, 128)) * slot_mask
-            tmeta[aligned(s * CAP, CAP, CAP), :] = line.astype(BF16)
-
-        loop(0, 32, stretch)
+        def stretch(b, g=g):
+            for i in range(8):
+                s = 8 * b + i
+                dx, dy, dz = offset(g * 16 + 4 * b + i // 2)
+                sx, sy = lax.rem(xi + 4 - dx, 4), lax.rem(yi + 4 - dy, 4)
+                source = meta[sy * 2 + i % 2, sx, lax.rem(lat + 4 - dz, 4)]
+                line = jnp.broadcast_to(source, (CAP, 128)) * slot_mask
+                tmeta[aligned(s * CAP, CAP, CAP), :] = line.astype(BF16)
+
+        loop(0, 4, stretch)
         await_bytes(vals.at[pl.ds(g * 16, 16)], a2a_recv.at[g])
 
-        def embed_block(b, g=g):
-            at = aligned(b * 256, 256, 256)
-            of = aligned(g * GROUP + b * 256, 256, 256)
+        for b in range(4):
+            at = slice(b * 256, b * 256 + 256)
+            of = slice(g * GROUP + b * 256, g * GROUP + b * 256 + 256)
             wide = dot(tmeta[at, :], spread)
             colb[of, :] = wide[:, 0:128].astype(BF16)
             rowb[of, :] = wide[:, 384:512].astype(BF16)
@@ -280,9 +281,8 @@
             ).astype(BF16)
             w = jnp.exp(radius * decay)
             weight[of, :] = w
-            ew[at, :] = (dot(vals[pl.ds(g * 16 + 4 * b, 4)].reshape(256, VALS), embed_w[...]) * w).astype(BF16)
-
-        loop(0, 4, embed_block)
+            ew[at, :] = (dot(vals[g * 16 + 4 * b : g * 16 + 4 * b + 4].reshape(256, VALS), embed_w[...]) * w).astype(BF16)
+
         both = lax.dot_general(pick, tmeta[...], NT, preferred_element_type=F32)
         colhot[...] = jnp.where(
             both[0:COLS] == iota((COLS, GROUP), 0).astype(F32), 1.0, 0.0
@@ -290,37 +290,35 @@
         rowl[...] = both[COLS : COLS + 16]
         counts[...] += dot(colhot[...], rk[...])
 
-        def place(pair):
-            hot = colhot[...].reshape(8, 16, GROUP)
-            halves = []
-            for h in range(2):
-                r = (2 * pair + h).astype(F32)
-                mask = jnp.where(rowl[...] == r, 1.0, 0.0).astype(BF16)
-                halves.append((hot * mask[None]).reshape(COLS, GROUP))
-            at = aligned(pair * 256, 256, 256)
-            placed[at, :] += dot(jnp.concatenate(halves, axis=0), ew[...])
-
-        loop(0, 8, place)
-
-    tally = counts[...].astype(BF16)
+        hot = colhot[...].reshape(8, 16, GROUP)
+        for b in range(4):
+            rows = []
+            for r in range(4 * b, 4 * b + 4):
+                mask = jnp.where(rowl[...] == float(r), 1.0, 0.0).astype(BF16)
+                rows.append((hot * mask[None]).reshape(COLS, GROUP))
+            at = slice(b * 512, b * 512 + 512)
+            placed[at, :] += dot(jnp.concatenate(rows, axis=0), ew[...])
+
     kind = lax.rem(iota((256, CH), 0), 16)
     half_u, half_v = 2 * lax.div(kind, 4) + 1, 2 * lax.rem(kind, 4) + 1
     table = jnp.exp((half_u * half_u + half_v * half_v).astype(F32) * decay)
     table_hi = table.astype(BF16)
     table_lo = (table - table_hi.astype(F32)).astype(BF16)
-
-    def base_row(r):
-        own = lax.div(iota((256, CH), 0), 16) == r
-        hi = jnp.where(own, table_hi.astype(F32), 0.0).astype(BF16)
-        lo = jnp.where(own, table_lo.astype(F32), 0.0).astype(BF16)
-        recip = 1.0 / (dot(tally, hi) + dot(tally, lo) + 1.0)
-        inv[r] = recip
-        value = (placed[aligned(r * COLS, COLS, COLS), :] * recip).astype(BF16)
-        base[r] = value
+    tables = jnp.concatenate([table_hi, table_lo], axis=0)
+    row_of_lane = lax.div(iota((COLS, 256), 1), 16)
+    for b in range(4):
+        rows = []
+        for r in range(4 * b, 4 * b + 4):
+            rows.append(jnp.where(row_of_lane == r, counts[...], 0.0).astype(BF16))
+        tally = jnp.concatenate(rows, axis=0)
+        recip = 1.0 / (dot(jnp.concatenate([tally, tally], axis=1), tables) + 1.0)
+        at = slice(4 * b, 4 * b + 4)
+        inv[at] = grid4(recip)
+        value = (placed[b * 512 : b * 512 + 512, :] * recip).astype(BF16)
+        base[at] = grid4(value)
         x = value.astype(F32)
-        act_zero[r] = (x * sigmoid(x)).astype(BF16)
-
-    loop(0, ROWS, base_row)
+        act_zero[at] = grid4((x * sigmoid(x)).astype(BF16))
+
     halo_start(act_zero, 1)
     widen(act_zero, x3_act)
     turn_weights(0)
@@ -342,13 +340,11 @@
     halo_start(act_one, 3)
 
     def kernel_grad(act_t, x3, k):
-        def body(p):
-            block = dot(act_t[...], x3[pl.ds(2 - p, ROWS)].reshape(CELLS, 3 * CH))
+        for p in range(3):
+            block = dot(act_t[...], x3[2 - p : 2 - p + ROWS].reshape(CELLS, 3 * CH))
             for q in range(3):
-                at = aligned((k * 9 + 3 * p + q) * CH, CH, CH)
-                grads[at, :] = block[:, (2 - q) * CH : (3 - q) * CH].astype(BF16)
-
-        loop(0, 3, body)
+                at = (k * 9 + 3 * p + q) * CH
+                grads[at : at + CH, :] = block[:, (2 - q) * CH : (3 - q) * CH].astype(BF16)
 
     turn_act(act_one, act_t)
     kernel_grad(act_t, x3_cot, 1)
@@ -435,7 +431,7 @@
         x = tile4(base[rows]).astype(F32)
         s = sigmoid(x)
         grad = tile4(gmid[rows]).astype(F32) + acc * (s * (1.0 + x * (1.0 - s)))
-        gp[aligned(rows.start * COLS, 4 * COLS, 4 * COLS), :] = (
+        gp[rows.start * COLS : rows.stop * COLS, :] = (
             grad * tile4(inv[rows])
         ).astype(BF16)
 
@@ -451,9 +447,10 @@
         return remote(vg.at[j], relay.at[chip], vg_send, vg_recv, sz, sx * 8 + sy * 2 + ci)
 
     def gather(b):
-        at = aligned(b * 256, 256, 256)
+        at = slice(b * 512, b * 512 + 512)
+        chips = slice(b * 8, b * 8 + 8)
         hot = jnp.where(
-            colb[at, :].astype(F32) == iota((256, COLS), 1).astype(F32), 1.0, 0.0
+            colb[at, :].astype(F32) == iota((512, COLS), 1).astype(F32), 1.0, 0.0
         ).astype(BF16)
         row_of = rowb[at, :]
         pieces = [
@@ -461,30 +458,29 @@
         ]
         found = dot(jnp.concatenate(pieces, axis=1), gp[...])
         grad = (found * weight[at, :]).astype(BF16)
-        vg[pl.ds(4 * b, 4)] = dot(grad, embed_t[...]).astype(BF16).reshape(4, 2, CAP, VALS)
-        own = vals[pl.ds(4 * b, 4)].reshape(256, VALS)
+        vg[chips] = dot(grad, embed_t[...]).astype(BF16).reshape(8, 2, CAP, VALS)
+        own = vals[chips].reshape(512, VALS)
         esum[...] += lax.dot_general(own, grad, TN, preferred_element_type=F32)
+        for j in range(8 * b, 8 * b + 8):
+            if j == 0:
+                pltpu.make_async_copy(vg.at[0], relay.at[chip], vg_recv).start()
+            else:
+                vg_copy(j).start()
 
     gather(0)
-    pltpu.make_async_copy(vg.at[0], relay.at[chip], vg_recv).start()
-    for j in range(1, 4):
-        vg_copy(j).start()
-
-    def gather_send(b):
-        gather(b)
-        for s in range(4):
-            vg_copy(b * 4 + s).start()
-
-    loop(1, 6, gather_send)
+    gather(1)
+    gather(2)
     ar_finish(1)
     ar_start(2)
-    loop(6, 9, gather_send)
+    gather(3)
     ar_finish(2)
     ar_start(3)
-    loop(9, 12, gather_send)
+    gather(4)
+    gather(5)
     ar_finish(3)
     ar_start(4)
-    loop(12, 16, gather_send)
+    gather(6)
+    gather(7)
     ar_finish(4)
     ar_start(5)
 
@@ -566,26 +562,19 @@
     grads_copy.wait()
 
 
-def scaled(grads_ref, out_ref):
-    out_ref[...] = grads_ref[...].astype(F32) * (1.0 / 512.0)
-
-
 def on_device(
     obs_values, obs_cells, obs_subcell, slot_counts, sharpness, embed_weight, conv_weight, cotangent
 ):
-    cells = obs_cells.reshape(DEVICES, 1, CAP)
-    subs = obs_subcell.reshape(DEVICES, 1, CAP)
-    spread = (DEVICES, 4, CAP)
-    live = lax.broadcasted_iota(jnp.int32, spread, 2) < slot_counts.reshape(DEVICES, 1, 1)
-    field = lax.broadcasted_iota(jnp.int32, spread, 1)
+    cells = obs_cells.reshape(DEVICES, CAP)
+    subs = obs_subcell.reshape(DEVICES, CAP)
+    live = lax.broadcasted_iota(jnp.int32, (DEVICES, CAP), 1) < slot_counts.reshape(DEVICES, 1)
     i, j = subs >> 3, subs & 7
     u = jnp.where(i >= 4, i - 4, 3 - i)
     v = jnp.where(j >= 4, j - 4, 3 - j)
     row = cells >> 7
     radius = (2 * u + 1) * (2 * u + 1) + (2 * v + 1) * (2 * v + 1)
     column = jnp.where(live, cells & 127, 255)
-    rest = jnp.where(field == 1, row * 16 + u * 4 + v, jnp.where(field == 2, radius, row))
-    meta = jnp.where(field == 0, column, rest).astype(F32)
+    meta = jnp.concatenate([column, row * 16 + u * 4 + v, radius, row], axis=1).astype(F32)
     anywhere = pl.BlockSpec(memory_space=pl.ANY)
     vmem = pl.BlockSpec(memory_space=pltpu.VMEM)
     grid = (ROWS, COLS, CH)
@@ -685,13 +674,7 @@
         conv_weight.reshape(2, 3, 3 * CH, CH),
         cotangent,
     )
-    conv_grads = pl.pallas_call(
-        scaled,
-        grid=(6,),
-        out_shape=jax.ShapeDtypeStruct((3 * PART, CH), F32),
-        in_specs=[pl.BlockSpec((HALF, CH), lambda i: (i, 0))],
-        out_specs=pl.BlockSpec((HALF, CH), lambda i: (i, 0)),
-    )(grads)
+    conv_grads = grads.astype(F32) * (1.0 / 512.0)
     return (
         encoded,
         value_grads.reshape(OBS, VALS),

time: 138 us -> 122 us (0.88)
  Pallas kernels: 127 us -> 109 us
  other arithmetic: 3.67 us -> 7.58 us
  local copies, waits for them, and re-layouts: 5.63 us -> 3.71 us
    pallas_call x1, Pallas kernels: 122 us -> 109 us  [on_device(): pl.pallas_call(kernel, out_shape=(jax.ShapeDtypeStruct(grid, BF16), jax.S...]
    pallas_call x1 -> x0, Pallas kernels: 5.33 us -> none  [on_device(): pl.pallas_call(scaled, grid=(6,), out_shape=jax.ShapeDtypeStruct((3 * PAR...]
    mul x1, other arithmetic: 0.73 us -> 4.31 us  [on_device(): conv_grads = grads.astype(F32) * (1.0 / 512.0)]
where the time goes in v2:
time: 122 us; the launch traced here: 121 us
  Pallas kernels  109 us (89%)
  other arithmetic  7.58 us (6%)
  local copies, waits for them, and re-layouts  3.71 us (3%)
    pallas_call x1, Pallas kernels, on_device(): pl.pallas_call(kernel, out_shape=(jax.ShapeDtypeStruct(grid, BF16), jax.S...  109 us
    mul x1, other arithmetic, on_device(): conv_grads = grads.astype(F32) * (1.0 / 512.0)  4.31 us
    unnamed x10, local copies, waits for them, and re-layouts  3.12 us

profile of v2, /device:TPU:1, one launch (start us, length us, event | category | flops | bytes accessed | tf_op | source)
XLA Modules:
  0.0 121.3 jit_solution(5662095858012400004)
XLA Ops:
  0.6 0.5 broadcast.234
  1.1 1.3 %reduce.3 = s32[128]{0:T(128)S(1)} reduce(s32[1,128]{1,0:T(1,128)} %param.11, s32[]{:T(128)} %broadcast.234), dimensions={0}, to_apply=%param.11.reduce_sub_computation.3 | reduce | bytes 1028 | tf_op args[3]
  2.5 0.1 lt.16
  2.6 0.8 broadcast_and_fusion
  3.3 0.1 and.33
  3.4 0.1 fusion
  3.5 0.1 concatenate.19
  3.6 0.1 concatenate.20
  3.8 0.1 concatenate.21
  3.9 1.1 add_convert_fusion.meta_in
  5.0 109.3 %shard_map.111 = (bf16[16,128,256]{2,1,0:T(8,128)(2,1)}, bf16[64,2,32,128]{3,2,1,0:T(8,128)(2,1)}, bf16[4608,256]{1,0:T(8,128)(2,1)}, f32[128,256]{1,0:T(8,128)}) custom-call(bf16[64,2,32,128]{3,2,1,0:T(8,128)(2,1)} %bitcast.10, f32[4,4,8,1,128]{4,3,2,1,0:T(1,128)} %add_convert_fusion.meta_in, f32[1,256]{1,0:T(1,128)} %bitcast.11, bf16[128,256]{1,0:T(8,128)(2,1)} %embed_w.1, ...), custom_call_target="tpu_custom_call" | custom-call | flops 30000001024 | bytes 20000000 | tf_op jit(solution)/shard_map/pallas_call | solution.py:652
  114.4 0.0 copy-start.1
  114.4 0.0 copy-start
  114.4 0.0 copy-start.2
  114.4 4.3 %convert_multiply_fusion = f32[4608,256]{1,0:T(8,128)} fusion(bf16[4608,256]{1,0:T(8,128)(2,1)} %get-tuple-element.10), kind=kLoop, calls=%fused_computation | loop fusion | flops 2359296 | bytes 7077888 | tf_op jit(solution)/shard_map/mul | solution.py:677
  118.7 0.0 copy-done.1
  118.7 1.0 copy.15
  119.7 0.0 copy-done
  119.7 1.0 copy.16
  120.6 0.0 copy-done.2
  120.6 0.7 copy.17
Async XLA Ops:
  114.4 4.3 %copy-start.1 = (bf16[16,128,256]{2,1,0:T(8,128)(2,1)S(1)}, bf16[16,128,256]{2,1,0:T(8,128)(2,1)}, u32[]{:S(2)}) copy-start(bf16[16,128,256]{2,1,0:T(8,128)(2,1)} %get-tuple-element.20) | copy-start | bytes 3145732
  114.4 5.3 %copy-start = (bf16[64,2,32,128]{3,2,1,0:T(8,128)(2,1)S(1)}, bf16[64,2,32,128]{3,2,1,0:T(8,128)(2,1)}, u32[]{:S(2)}) copy-start(bf16[64,2,32,128]{3,2,1,0:T(8,128)(2,1)} %get-tuple-element.9) | copy-start | bytes 3145732
  114.4 6.3 %copy-start.2 = (f32[128,256]{1,0:T(8,128)S(1)}, f32[128,256]{1,0:T(8,128)}, u32[]{:S(2)}) copy-start(f32[128,256]{1,0:T(8,128)} %get-tuple-element.23) | copy-start | bytes 393220

commit v3 on v2

--- a/solution.py
+++ b/solution.py
@@ -28,7 +28,7 @@
 
 
 def sigmoid(x):
-    return 1.0 / (1.0 + jnp.exp(-x))
+    return 0.5 + 0.5 * jnp.tanh(0.5 * x)
 
 
 def remote(src, dst, send, recv, lat, lon):
@@ -59,10 +59,10 @@
 
 
 def kernel(
-    obs_in, meta_in, sharp, embed_w, conv_in, cot_in,
+    obs_in, cells, subs, live_counts, sharp, embed_w, conv_in, cot_in,
     enc_out, vg_out, grads_out, embed_out,
-    vals, queue, relay, meta_z, meta_x, meta, tmeta, colb, rowb, weight, ew, rk, colhot, rowl, placed, counts, inv,
-    cot, conv_w, conv_t, embed_t, back, base, act_zero, mid, act_one, gmid, gp, act_t, zero_t,
+    vals, queue, relay, meta_own, meta_z, meta_x, meta, tmeta, colb, rowb, weight, ew, rk, colhot, rowl, placed, counts, inv,
+    cot, conv_w, embed_t, back, bend, base, act_zero, mid, act_one, gmid, gp, act_t, zero_t,
     x3_act, x3_cot, x3_mid, hrow, hcol, strip, stripf,
     vg, grads, total, p0, s1, p1, s2, p2, s3, p3, esum, pe, qe, etotal, enc,
     local_sem, pair_send, pair_recv, a2a_send, a2a_recv, meta_send, meta_recv, vg_send, vg_recv,
@@ -81,6 +81,8 @@
         g, dx, dy = lax.div(j, 16), lax.rem(lax.div(j, 4), 4), lax.rem(j, 4)
         return dx, dy, lax.rem(g + 8 - dx - dy, 4)
 
+    barrier = pltpu.get_barrier_semaphore()
+
     cot_copy = pltpu.make_async_copy(cot_in, cot, local_sem.at[0])
     cot_copy.start()
     pair_own = pltpu.make_async_copy(obs_in.at[:, ci], queue.at[:, ci], local_sem.at[4])
@@ -88,25 +90,34 @@
     pair_other = remote(
         obs_in.at[:, 1 - ci], queue.at[:, ci], pair_send.at[0], pair_recv.at[0], lat, other_core
     )
-    pair_other.start()
+
+    def greet(j):
+        tlat, tlon = lax.rem(lat + lax.div(j, N_LON), N_LAT), lax.rem(lon + lax.rem(j, N_LON), N_LON)
+        pl.semaphore_signal(
+            barrier, inc=1, device_id=(tlat, tlon), device_id_type=pl.DeviceIdType.MESH
+        )
+
+    loop(1, DEVICES, greet)
 
     def meta_copies(stage):
         copies = []
         for d in range(1, 8 if stage == 2 else 4):
             if stage == 0:
                 c = lax.rem(lat + d, 4)
-                src, dst, target = meta_in.at[c], meta_z.at[lat], (c, lon)
+                src, dst, target = meta_own.at[:, pl.ds(c * 8, 8)], meta_z.at[lat], (c, lon)
             elif stage == 1:
                 c = lax.rem(xi + d, 4)
-                src, dst, target = meta_z.at[:, c], meta_x.at[xi], (lat, c * 8 + yc)
+                src, dst = meta_z.at[:, :, pl.ds(c * 2, 2)], meta_x.at[xi]
+                target = (lat, c * 8 + yc)
             else:
                 c = lax.rem(yc + d, 8)
-                src, dst, target = meta_x.at[:, :, c], meta.at[yc], (lat, xi * 8 + c)
+                src, dst = meta_x.at[:, :, lax.rem(c, 4), lax.div(c, 4)], meta.at[yc]
+                target = (lat, xi * 8 + c)
             copies.append(remote(src, dst, meta_send.at[stage], meta_recv.at[stage], *target))
         own = (
-            (meta_in.at[lat], meta_z.at[lat]),
-            (meta_z.at[:, xi], meta_x.at[xi]),
-            (meta_x.at[:, :, yc], meta.at[yc]),
+            (meta_own.at[:, pl.ds(lat * 8, 8)], meta_z.at[lat]),
+            (meta_z.at[:, :, pl.ds(xi * 2, 2)], meta_x.at[xi]),
+            (meta_x.at[:, :, lax.rem(yc, 4), lax.div(yc, 4)], meta.at[yc]),
         )[stage]
         copies.append(pltpu.make_async_copy(*own, meta_recv.at[stage]))
         return copies
@@ -121,7 +132,32 @@
     def meta_sent(stage):
         await_bytes((meta_z, meta_x, meta)[stage].at[pl.ds(0, (3, 3, 7)[stage])], meta_send.at[stage])
 
-    meta_start(0)
+    line, lane = iota((32, 128), 0), iota((32, 128), 1)
+    own_four = jnp.where(lax.div(lane, 4) == line, live_counts[...].astype(F32), 0.0).astype(BF16)
+    to_slots = jnp.where(
+        lax.rem(iota((128, 128), 0), 4) == lax.div(iota((128, 128), 1), 32), 1.0, 0.0
+    ).astype(BF16)
+    live = lax.rem(lane, 32).astype(F32) < dot(own_four, to_slots)
+    cell, sub = cells[...], subs[...]
+    u, v = sub >> 3, sub & 7
+    u = jnp.where(u >= 4, u - 4, 3 - u)
+    v = jnp.where(v >= 4, v - 4, 3 - v)
+    row = cell >> 7
+    fields = [
+        jnp.where(live, (cell & 127).astype(F32), 255.0),
+        (row * 16 + u * 4 + v).astype(F32),
+        ((2 * u + 1) * (2 * u + 1) + (2 * v + 1) * (2 * v + 1)).astype(F32),
+        row.astype(F32),
+    ]
+    for i in range(4):
+        mixed = jnp.zeros((32, 128), F32)
+        for f in range(4):
+            shift = (f - i) * 32 % 128
+            turned_field = pltpu.roll(fields[f], shift, 1) if shift else fields[f]
+            mixed = jnp.where(lax.div(lane, 32) == f, turned_field, mixed)
+        for r in range(32):
+            meta_own[i, r] = mixed[r : r + 1, :]
+
     conv_copy = pltpu.make_async_copy(conv_in, conv_w, local_sem.at[1])
     conv_copy.start()
 
@@ -150,16 +186,18 @@
             for i, (s, d, a, b) in enumerate(pieces)
         ]
 
-    def halo_start(src, k):
+    def halo_pack(src, k):
         for r in range(ROWS):
             stripf[0, r : r + 1, :] = src[r, 0:16, :].astype(F32)[0:1, :]
             stripf[1, r : r + 1, :] = src[r, COLS - 16 : COLS, :].astype(F32)[15:16, :]
         strip[k, 0] = stripf[0].astype(BF16)
         strip[k, 1] = stripf[1].astype(BF16)
+
+    def halo_start(src, k):
         for copy in halo_copies(src, k):
             copy.start()
 
-    def widen(src, x3):
+    def widen(src, x3, low=0, high=4):
         def body(b):
             for i in range(4):
                 r = 4 * b + i
@@ -168,7 +206,7 @@
                 x3[r + 1, :, CH : 2 * CH] = src[r]
                 x3[r + 1, :, 2 * CH : 3 * CH] = pltpu.roll(row, COLS - 1, 0).astype(BF16)
 
-        loop(0, ROWS // 4, body)
+        loop(low, high, body)
 
     def halo_finish(src, k, x3):
         for copy in halo_copies(src, k):
@@ -199,48 +237,57 @@
                 spot == COLS - 1, rcorner, pltpu.roll(row, COLS - 1, 0)
             ).astype(BF16)
 
-    def conv(x3, w, k, finish, low=0, high=4):
-        taps = w[k].reshape(9 * CH, CH)
+    def conv(x3, k, finish, flip=False, low=0, high=4):
+        if flip:
+            taps = [
+                conv_w[k, 2 - p, (2 - q) * CH : (3 - q) * CH, :] for p in range(3) for q in range(3)
+            ]
+            taps = jnp.concatenate(taps, axis=1)
+        else:
+            taps = conv_w[k].reshape(9 * CH, CH)
         for b in range(low, high):
             near = [x3[4 * b + p : 4 * b + p + 4].reshape(4 * COLS, 3 * CH) for p in range(3)]
-            finish(slice(4 * b, 4 * b + 4), dot(jnp.concatenate(near, axis=1), taps))
+            near = jnp.concatenate(near, axis=1)
+            if flip:
+                acc = lax.dot_general(near, taps, NT, preferred_element_type=F32)
+            else:
+                acc = dot(near, taps)
+            finish(slice(4 * b, 4 * b + 4), acc)
 
     def tile4(x):
         return x.reshape(4 * COLS, CH)
 
     def grid4(x):
         return x.reshape(4, COLS, CH)
-
-    def turn_weights(k):
-        for p in range(3):
-            for q in range(3):
-                block = conv_w[k, 2 - p, (2 - q) * CH : (3 - q) * CH, :]
-                conv_t[k, p, q * CH : (q + 1) * CH, :] = block.T
 
     def turn_act(act, act_t):
         for r in range(ROWS):
             act_t[:, r * COLS : (r + 1) * COLS] = act[r].T
 
     cot_copy.wait()
+    halo_pack(cot, 0)
+    pl.semaphore_wait(barrier, DEVICES - 1)
+    pair_other.start()
+    meta_start(0)
     halo_start(cot, 0)
+    widen(cot, x3_cot, 0, 2)
     meta_wait(0)
     meta_start(1)
+    widen(cot, x3_cot, 2, 4)
+    meta_wait(1)
+    meta_start(2)
     pair_own.wait()
     pair_other.wait()
     pltpu.make_async_copy(queue.at[chip], vals.at[0], a2a_recv.at[0]).start()
     loop(1, 64, send_slot)
-    widen(cot, x3_cot)
-    meta_wait(1)
-    meta_start(2)
     conv_copy.wait()
-    turn_weights(1)
     embed_t[...] = embed_w[...].T
     halo_finish(cot, 0, x3_cot)
 
     def keep_back(rows, acc):
         back[rows] = grid4(acc)
 
-    conv(x3_cot, conv_t, 1, keep_back)
+    conv(x3_cot, 1, keep_back, flip=True)
     meta_wait(2)
 
     placed[...] = jnp.zeros_like(placed)
@@ -317,11 +364,13 @@
         value = (placed[b * 512 : b * 512 + 512, :] * recip).astype(BF16)
         base[at] = grid4(value)
         x = value.astype(F32)
-        act_zero[at] = grid4((x * sigmoid(x)).astype(BF16))
-
+        s = sigmoid(x)
+        act_zero[at] = grid4((x * s).astype(BF16))
+        bend[at] = grid4(s * (1.0 + x * (1.0 - s)))
+
+    halo_pack(act_zero, 1)
     halo_start(act_zero, 1)
     widen(act_zero, x3_act)
-    turn_weights(0)
     turn_act(act_zero, zero_t)
     halo_finish(act_zero, 1, x3_act)
 
@@ -335,22 +384,19 @@
         grad = tile4(cot[rows]).astype(F32) + tile4(back[rows]) * slope
         gmid[rows] = grid4(grad.astype(BF16))
 
-    conv(x3_act, conv_w, 0, keep_mid)
+    conv(x3_act, 0, keep_mid)
+    halo_pack(gmid, 2)
     halo_start(gmid, 2)
+    halo_pack(act_one, 3)
     halo_start(act_one, 3)
 
     def kernel_grad(act_t, x3, k):
         for p in range(3):
             block = dot(act_t[...], x3[2 - p : 2 - p + ROWS].reshape(CELLS, 3 * CH))
             for q in range(3):
-                at = (k * 9 + 3 * p + q) * CH
-                grads[at : at + CH, :] = block[:, (2 - q) * CH : (3 - q) * CH].astype(BF16)
-
-    turn_act(act_one, act_t)
-    kernel_grad(act_t, x3_cot, 1)
-    widen(gmid, x3_mid)
-    halo_finish(gmid, 2, x3_mid)
-    kernel_grad(zero_t, x3_mid, 0)
+                for h in range(2):
+                    at, lanes = (6 * p + 2 * q + h) * CH, (2 - q) * CH + h * 128
+                    grads[k, at : at + CH, :] = block[:, lanes : lanes + 128].astype(BF16)
 
     coords = {"x": xi, "y": yi, "z": lat}
     orders = (("x", "y", "z"), ("y", "z", "x"), ("z", "x", "y"))
@@ -362,82 +408,93 @@
     def turned(axis, d):
         return lax.rem(coords[axis] + d, 4)
 
-    def part_copies(stage):
+    def part_copies(k, stage):
         copies = []
         for a, order in enumerate(orders):
             own = a * PART + ci * HALF
-            sems = lambda d: (ar_send.at[stage, a, d], ar_recv.at[stage, a, d])
+            sems = lambda d: (ar_send.at[k, stage, a, d], ar_recv.at[k, stage, a, d])
             quarter = own + coords[order[0]] * QUARTER
             shard = quarter + coords[order[1]] * SHARD
             if stage == 0:
-                src = grads.at[aligned(a * PART + (1 - ci) * HALF, HALF, 16)]
-                copies.append(remote(src, p0.at[a], *sems(0), lat, other_core))
+                src = grads.at[k, aligned(a * PART + (1 - ci) * HALF, HALF, 16)]
+                copies.append(remote(src, p0.at[k, a], *sems(0), lat, other_core))
             elif stage == 6:
-                piece = total.at[aligned(own, HALF, 16)]
+                piece = total.at[k, aligned(own, HALF, 16)]
                 copies.append(remote(piece, piece, *sems(0), lat, other_core))
             else:
                 axis = order[{1: 0, 2: 1, 3: 2, 4: 1, 5: 0}[stage]]
                 for d in (1, 3, 2):
                     c = turned(axis, d)
                     if stage == 1:
-                        src, dst = s1.at[a, aligned(c * QUARTER, QUARTER, 16)], p1.at[a, d - 1]
+                        src = s1.at[k, a, aligned(c * QUARTER, QUARTER, 16)]
+                        dst = p1.at[k, a, d - 1]
                     elif stage == 2:
-                        src, dst = s2.at[a, aligned(c * SHARD, SHARD, 16)], p2.at[a, d - 1]
+                        src = s2.at[k, a, aligned(c * SHARD, SHARD, 16)]
+                        dst = p2.at[k, a, d - 1]
                     elif stage == 3:
-                        src, dst = s3.at[a], p3.at[a, coords[axis]]
+                        src, dst = s3.at[k, a], p3.at[k, a, coords[axis]]
                     elif stage == 4:
-                        src = dst = total.at[aligned(shard, SHARD, 16)]
+                        src = dst = total.at[k, aligned(shard, SHARD, 16)]
                     else:
-                        src = dst = total.at[aligned(quarter, QUARTER, 16)]
+                        src = dst = total.at[k, aligned(quarter, QUARTER, 16)]
                     copies.append(remote(src, dst, *sems(d - 1), *along(axis, c)))
         return copies
 
-    def ar_start(stage):
-        for copy in part_copies(stage):
+    def ar_start(k, stage):
+        for copy in part_copies(k, stage):
             copy.start()
 
-    def ar_finish(stage):
-        for copy in part_copies(stage):
+    def ar_finish(k, stage):
+        for copy in part_copies(k, stage):
             copy.wait()
         for a, order in enumerate(orders):
             own = a * PART + ci * HALF
             if stage == 0:
-
-                def body(b, a=a, own=own):
-                    here = grads[aligned(own + b * QUARTER, QUARTER, 16), :].astype(F32)
-                    at = aligned(b * QUARTER, QUARTER, 16)
-                    s1[a, at, :] = (here + p0[a, at, :].astype(F32)).astype(BF16)
-
-                loop(0, 4, body)
+                here = grads[k, aligned(own, HALF, 16), :].astype(F32)
+                s1[k, a] = (here + p0[k, a].astype(F32)).astype(BF16)
             elif stage in (1, 2):
                 size = QUARTER if stage == 1 else SHARD
                 src, came, dst = (s1, p1, s2) if stage == 1 else (s2, p2, s3)
-                here = src[a, aligned(coords[order[stage - 1]] * size, size, 16), :].astype(F32)
+                at = aligned(coords[order[stage - 1]] * size, size, 16)
+                here = src[k, a, at, :].astype(F32)
                 for d in range(3):
-                    here += came[a, d].astype(F32)
-                dst[a] = here.astype(BF16)
+                    here += came[k, a, d].astype(F32)
+                dst[k, a] = here.astype(BF16)
             elif stage == 3:
-                p3[a, coords[order[2]]] = s3[a]
-                whole = p3[a, 0].astype(F32)
+                p3[k, a, coords[order[2]]] = s3[k, a]
+                whole = p3[k, a, 0].astype(F32)
                 for d in range(1, 4):
-                    whole += p3[a, d].astype(F32)
+                    whole += p3[k, a, d].astype(F32)
                 quarter = own + coords[order[0]] * QUARTER
                 at = aligned(quarter + coords[order[1]] * SHARD, SHARD, 16)
-                total[at, :] = whole.astype(BF16)
-
-    ar_start(0)
+                total[k, at, :] = whole.astype(BF16)
+
+    def ar_step(k, stage):
+        ar_finish(k, stage)
+        ar_start(k, stage + 1)
+
+    def ar_leave(k):
+        return pltpu.make_async_copy(total.at[k], grads_out.at[k], local_sem.at[3 if k else 6])
+
+    turn_act(act_one, act_t)
+    kernel_grad(act_t, x3_cot, 1)
+    ar_start(1, 0)
+    widen(gmid, x3_mid)
+    halo_finish(gmid, 2, x3_mid)
+    ar_step(1, 0)
+    kernel_grad(zero_t, x3_mid, 0)
+    ar_start(0, 0)
 
     def keep_gp(rows, acc):
-        x = tile4(base[rows]).astype(F32)
-        s = sigmoid(x)
-        grad = tile4(gmid[rows]).astype(F32) + acc * (s * (1.0 + x * (1.0 - s)))
+        grad = tile4(gmid[rows]).astype(F32) + acc * tile4(bend[rows])
         gp[rows.start * COLS : rows.stop * COLS, :] = (
             grad * tile4(inv[rows])
         ).astype(BF16)
 
-    conv(x3_mid, conv_t, 0, keep_gp)
-    ar_finish(0)
-    ar_start(1)
+    conv(x3_mid, 0, keep_gp, flip=True, low=0, high=2)
+    ar_step(1, 1)
+    ar_step(0, 0)
+    conv(x3_mid, 0, keep_gp, flip=True, low=2, high=4)
 
     esum[...] = jnp.zeros_like(esum)
 
@@ -469,20 +526,19 @@
 
     gather(0)
     gather(1)
+    ar_step(1, 2)
     gather(2)
-    ar_finish(1)
-    ar_start(2)
+    ar_step(0, 1)
     gather(3)
-    ar_finish(2)
-    ar_start(3)
+    ar_step(1, 3)
     gather(4)
+    ar_step(0, 2)
     gather(5)
-    ar_finish(3)
-    ar_start(4)
+    ar_step(1, 4)
     gather(6)
+    ar_step(0, 3)
     gather(7)
-    ar_finish(4)
-    ar_start(5)
+    ar_step(0, 4)
 
     member = yc
     column = xi * 4 + lat
@@ -515,11 +571,12 @@
     embed_start(0)
     widen(act_one, x3_act)
     halo_finish(act_one, 3, x3_act)
+    ar_step(1, 5)
 
     def keep_enc(rows, acc):
         enc[rows] = grid4((tile4(mid[rows]).astype(F32) + acc).astype(BF16))
 
-    conv(x3_act, conv_w, 1, keep_enc, 0, 2)
+    conv(x3_act, 1, keep_enc, low=0, high=2)
     embed_wait(0)
     own_rows = aligned(member * 16, 16, 16)
     mine = esum[own_rows, :]
@@ -527,7 +584,10 @@
         mine += pe[d]
     esum[own_rows, :] = mine
     embed_start(1)
-    conv(x3_act, conv_w, 1, keep_enc, 2, 4)
+    ar_step(0, 5)
+    ar_finish(1, 6)
+    ar_leave(1).start()
+    conv(x3_act, 1, keep_enc, low=2, high=4)
     enc_copy = pltpu.make_async_copy(enc, enc_out, local_sem.at[2])
     enc_copy.start()
     embed_wait(1)
@@ -537,8 +597,6 @@
         whole += qe[d]
     etotal[own_rows, :] = whole
     embed_start(2)
-    ar_finish(5)
-    ar_start(6)
     await_bytes(relay, vg_recv)
     vg_own = pltpu.make_async_copy(relay.at[:, ci], vg_out.at[:, ci], local_sem.at[5])
     vg_own.start()
@@ -546,9 +604,8 @@
         relay.at[:, 1 - ci], vg_out.at[:, ci], pair_send.at[1], pair_recv.at[1], lat, other_core
     )
     vg_other.start()
-    ar_finish(6)
-    grads_copy = pltpu.make_async_copy(total, grads_out, local_sem.at[3])
-    grads_copy.start()
+    ar_finish(0, 6)
+    ar_leave(0).start()
     embed_wait(2)
     embed_out[...] = etotal[...] * (1.0 / 512.0)
     for g in range(4):
@@ -559,22 +616,49 @@
     vg_own.wait()
     vg_other.wait()
     enc_copy.wait()
-    grads_copy.wait()
+    ar_leave(1).wait()
+    ar_leave(0).wait()
+
+
+def hand_over(
+    enc_in, vg_in, grads_in, embed_in, enc_out, vg_out, grads_out, embed_out,
+    enc, vg, embed, narrow, wide, in_sem, out_sem,
+):
+    steps = []
+    for i in range(18):
+        src, dst = slice(i % 9 * 2 * CH, (i % 9 + 1) * 2 * CH), slice(i * CH, i * CH + CH)
+        k = i // 9
+        steps.append(
+            (grads_in.at[k, src], narrow.at[k, src], wide.at[dst], grads_out.at[dst], (k, src, dst))
+        )
+    for i in range(2):
+        at = slice(i * 8, i * 8 + 8)
+        steps.append((enc_in.at[at], enc.at[at], enc.at[at], enc_out.at[at], None))
+        at = slice(i * 32, i * 32 + 32)
+        steps.append((vg_in.at[at], vg.at[at], vg.at[at], vg_out.at[at], None))
+    steps.append((embed_in, embed, embed, embed_out, None))
+    moves = [
+        pltpu.make_async_copy(step[0], step[1], in_sem.at[i]) for i, step in enumerate(steps)
+    ]
+    for move in moves:
+        move.start()
+    results = []
+    for i, (_, _, src, dst, at) in enumerate(steps):
+        moves[i].wait()
+        if at is not None:
+            k, rows, to = at
+            for h in range(2):
+                half = slice(rows.start + h * CH, rows.start + h * CH + CH)
+                wide[to, h * 128 : h * 128 + 128] = narrow[k, half, :].astype(F32) * (1.0 / 512.0)
+        results.append(pltpu.make_async_copy(src, dst, out_sem.at[i]))
+        results[i].start()
+    for copy in results:
+        copy.wait()
 
 
 def on_device(
     obs_values, obs_cells, obs_subcell, slot_counts, sharpness, embed_weight, conv_weight, cotangent
 ):
-    cells = obs_cells.reshape(DEVICES, CAP)
-    subs = obs_subcell.reshape(DEVICES, CAP)
-    live = lax.broadcasted_iota(jnp.int32, (DEVICES, CAP), 1) < slot_counts.reshape(DEVICES, 1)
-    i, j = subs >> 3, subs & 7
-    u = jnp.where(i >= 4, i - 4, 3 - i)
-    v = jnp.where(j >= 4, j - 4, 3 - j)
-    row = cells >> 7
-    radius = (2 * u + 1) * (2 * u + 1) + (2 * v + 1) * (2 * v + 1)
-    column = jnp.where(live, cells & 127, 255)
-    meta = jnp.concatenate([column, row * 16 + u * 4 + v, radius, row], axis=1).astype(F32)
     anywhere = pl.BlockSpec(memory_space=pl.ANY)
     vmem = pl.BlockSpec(memory_space=pltpu.VMEM)
     grid = (ROWS, COLS, CH)
@@ -584,8 +668,9 @@
         pltpu.VMEM((64, 2, CAP, VALS), BF16),
         pltpu.VMEM((64, 2, CAP, VALS), BF16),
         pltpu.VMEM((64, 2, CAP, VALS), BF16),
+        pltpu.VMEM((4, 32, 1, 128), F32),
         pltpu.VMEM((4, 4, 8, 1, 128), F32),
-        pltpu.VMEM((4, 4, 8, 1, 128), F32),
+        pltpu.VMEM((4, 4, 4, 2, 1, 128), F32),
         pltpu.VMEM((8, 4, 4, 1, 128), F32),
         pltpu.VMEM((GROUP, 128), BF16),
         pltpu.VMEM((OBS, 128), BF16),
@@ -600,8 +685,8 @@
         pltpu.VMEM(grid, F32),
         pltpu.VMEM(grid, BF16),
         pltpu.VMEM((2, 3, 3 * CH, CH), BF16),
-        pltpu.VMEM((2, 3, 3 * CH, CH), BF16),
         pltpu.VMEM((CH, VALS), BF16),
+        pltpu.VMEM(grid, F32),
         pltpu.VMEM(grid, F32),
         pltpu.VMEM(grid, BF16),
         pltpu.VMEM(grid, BF16),
@@ -619,21 +704,21 @@
         pltpu.VMEM((4, 2, 16, CH), BF16),
         pltpu.VMEM((2, 16, CH), F32),
         pltpu.VMEM((64, 2, CAP, VALS), BF16),
-        pltpu.VMEM((3 * PART, CH), BF16),
-        pltpu.VMEM((3 * PART, CH), BF16),
-        pltpu.VMEM((3, HALF, CH), BF16),
-        pltpu.VMEM((3, HALF, CH), BF16),
-        pltpu.VMEM((3, 3, QUARTER, CH), BF16),
-        pltpu.VMEM((3, QUARTER, CH), BF16),
-        pltpu.VMEM((3, 3, SHARD, CH), BF16),
-        pltpu.VMEM((3, SHARD, CH), BF16),
-        pltpu.VMEM((3, 4, SHARD, CH), BF16),
+        pltpu.VMEM((2, 3 * PART, 128), BF16),
+        pltpu.VMEM((2, 3 * PART, 128), BF16),
+        pltpu.VMEM((2, 3, HALF, 128), BF16),
+        pltpu.VMEM((2, 3, HALF, 128), BF16),
+        pltpu.VMEM((2, 3, 3, QUARTER, 128), BF16),
+        pltpu.VMEM((2, 3, QUARTER, 128), BF16),
+        pltpu.VMEM((2, 3, 3, SHARD, 128), BF16),
+        pltpu.VMEM((2, 3, SHARD, 128), BF16),
+        pltpu.VMEM((2, 3, 4, SHARD, 128), BF16),
         pltpu.VMEM((VALS, CH), F32),
         pltpu.VMEM((7, 16, CH), F32),
         pltpu.VMEM((16, 16, CH), F32),
         pltpu.VMEM((VALS, CH), F32),
         pltpu.VMEM(grid, BF16),
-        dma((6,)),
+        dma((7,)),
         dma((2,)),
         dma((2,)),
         dma((4,)),
@@ -644,8 +729,8 @@
         dma,
         dma((4, 8)),
         dma((4, 8)),
-        dma((7, 3, 3)),
-        dma((7, 3, 3)),
+        dma((2, 7, 3, 3)),
+        dma((2, 7, 3, 3)),
         dma((3, 15)),
         dma((3, 15)),
     ]
@@ -654,32 +739,54 @@
         out_shape=(
             jax.ShapeDtypeStruct(grid, BF16),
             jax.ShapeDtypeStruct((64, 2, CAP, VALS), BF16),
-            jax.ShapeDtypeStruct((3 * PART, CH), BF16),
+            jax.ShapeDtypeStruct((2, 3 * PART, 128), BF16),
             jax.ShapeDtypeStruct((VALS, CH), F32),
         ),
-        in_specs=[anywhere, anywhere, vmem, vmem, anywhere, anywhere],
+        in_specs=[anywhere, vmem, vmem, vmem, vmem, vmem, anywhere, anywhere],
         out_specs=(anywhere, anywhere, anywhere, vmem),
         scratch_shapes=scratch,
         compiler_params=pltpu.CompilerParams(
-            has_side_effects=True, vmem_limit_bytes=60 * 1024 * 1024
+            collective_id=0, has_side_effects=True, vmem_limit_bytes=60 * 1024 * 1024
         ),
         cost_estimate=pl.CostEstimate(
             flops=30_000_000_000, bytes_accessed=20_000_000, transcendentals=4_000_000
         ),
     )(
         obs_values.reshape(64, 2, CAP, VALS),
-        meta.reshape(4, 4, 8, 1, 128),
+        obs_cells.reshape(32, 128),
+        obs_subcell.reshape(32, 128),
+        slot_counts,
         sharpness.reshape(1, CH),
         embed_weight,
         conv_weight.reshape(2, 3, 3 * CH, CH),
         cotangent,
     )
-    conv_grads = grads.astype(F32) * (1.0 / 512.0)
+    encoded, value_grads, conv_grads, embed_grads = pl.pallas_call(
+        hand_over,
+        out_shape=(
+            jax.ShapeDtypeStruct(grid, BF16),
+            jax.ShapeDtypeStruct((64, 2, CAP, VALS), BF16),
+            jax.ShapeDtypeStruct((3 * PART, CH), F32),
+            jax.ShapeDtypeStruct((VALS, CH), F32),
+        ),
+        in_specs=[anywhere] * 4,
+        out_specs=(anywhere,) * 4,
+        scratch_shapes=[
+            pltpu.VMEM(grid, BF16),
+            pltpu.VMEM((64, 2, CAP, VALS), BF16),
+            pltpu.VMEM((VALS, CH), F32),
+            pltpu.VMEM((2, 3 * PART, 128), BF16),
+            pltpu.VMEM((3 * PART, CH), F32),
+            dma((23,)),
+            dma((23,)),
+        ],
+        compiler_params=pltpu.CompilerParams(vmem_limit_bytes=60 * 1024 * 1024),
+    )(encoded, value_grads, grads, embed_total)
     return (
         encoded,
         value_grads.reshape(OBS, VALS),
         conv_grads.reshape(2, 3, 3, CH, CH),
-        embed_total,
+        embed_grads,
     )
 
 

time: 122 us -> 106 us (0.87)
  other arithmetic: 7.58 us -> 0 us
  Pallas kernels: 109 us -> 105 us
  local copies, waits for them, and re-layouts: 3.71 us -> 0 us
    pallas_call x1, Pallas kernels: 109 us -> 101 us  [on_device(): pl.pallas_call(kernel, out_shape=(jax.ShapeDtypeStruct(grid, BF16), jax.S...]
    pallas_call x0 -> x1, Pallas kernels: none -> 4.76 us  [on_device(): pl.pallas_call(hand_over, out_shape=(jax.ShapeDtypeStruct(grid, BF16), ja...]
    mul x1 -> x0, other arithmetic: 4.31 us -> none  [on_device(): conv_grads = grads.astype(F32) * (1.0 / 512.0)]
    unnamed x10 -> x0, local copies, waits for them, and re-layouts: 3.12 us -> none
    unnamed x1 -> x0, other arithmetic: 1.32 us -> none
where the time goes in v3:
time: 106 us
  Pallas kernels  105 us (99%)
    pallas_call x1, Pallas kernels, on_device(): pl.pallas_call(kernel, out_shape=(jax.ShapeDtypeStruct(grid, BF16), jax.S...  101 us
    pallas_call x1, Pallas kernels, on_device(): pl.pallas_call(hand_over, out_shape=(jax.ShapeDtypeStruct(grid, BF16), ja...  4.76 us

profile of v3, /device:TPU:1, one launch (start us, length us, event | category | flops | bytes accessed | tf_op | source)
XLA Modules:
  0.0 106.3 jit_solution(12442058196315224455)
XLA Ops:
  0.6 100.7 %shard_map.111 = (bf16[16,128,256]{2,1,0:T(8,128)(2,1)}, bf16[64,2,32,128]{3,2,1,0:T(8,128)(2,1)}, bf16[2,4608,128]{2,1,0:T(8,128)(2,1)}, f32[128,256]{1,0:T(8,128)}) custom-call(bf16[64,2,32,128]{3,2,1,0:T(8,128)(2,1)} %bitcast.9, s32[32,128]{1,0:T(8,128)} %bitcast.11, s32[32,128]{1,0:T(8,128)} %bitcast.12, s32[1,128]{1,0:T(1,128)} %live_counts.1, ...), custom_call_target="tpu_custom_call" | custom-call | flops 30000001024 | bytes 20000000 | tf_op jit(solution)/shard_map/pallas_call | solution.py:737
  101.4 4.8 %shard_map.112 = (bf16[16,128,256]{2,1,0:T(8,128)(2,1)}, bf16[64,2,32,128]{3,2,1,0:T(8,128)(2,1)}, f32[4608,256]{1,0:T(8,128)}, f32[128,256]{1,0:T(8,128)}) custom-call(bf16[16,128,256]{2,1,0:T(8,128)(2,1)} %get-tuple-element.12.enc_in, bf16[64,2,32,128]{3,2,1,0:T(8,128)(2,1)} %get-tuple-element.13.vg_in, bf16[2,4608,128]{2,1,0:T(8,128)(2,1)} %get-tuple-element.14.grads_in, ...), custom_call_target="tpu_custom_call" | custom-call | tf_op jit(solution)/shard_map/pallas_call | solution.py:764

commit v4 on v3

--- a/solution.py
+++ b/solution.py
@@ -238,21 +238,23 @@
             ).astype(BF16)
 
     def conv(x3, k, finish, flip=False, low=0, high=4):
-        if flip:
-            taps = [
-                conv_w[k, 2 - p, (2 - q) * CH : (3 - q) * CH, :] for p in range(3) for q in range(3)
-            ]
-            taps = jnp.concatenate(taps, axis=1)
-        else:
-            taps = conv_w[k].reshape(9 * CH, CH)
-        for b in range(low, high):
-            near = [x3[4 * b + p : 4 * b + p + 4].reshape(4 * COLS, 3 * CH) for p in range(3)]
-            near = jnp.concatenate(near, axis=1)
-            if flip:
-                acc = lax.dot_general(near, taps, NT, preferred_element_type=F32)
-            else:
-                acc = dot(near, taps)
-            finish(slice(4 * b, 4 * b + 4), acc)
+        def body(pair):
+            for b in (2 * pair, 2 * pair + 1):
+                near = [x3[pl.ds(4 * b + p, 4)].reshape(4 * COLS, 3 * CH) for p in range(3)]
+                near = jnp.concatenate(near, axis=1)
+                if flip:
+                    taps = [
+                        conv_w[k, 2 - p, (2 - q) * CH : (3 - q) * CH, :]
+                        for p in range(3)
+                        for q in range(3)
+                    ]
+                    taps = jnp.concatenate(taps, axis=1)
+                    acc = lax.dot_general(near, taps, NT, preferred_element_type=F32)
+                else:
+                    acc = dot(near, conv_w[k].reshape(9 * CH, CH))
+                finish(pl.ds(4 * b, 4), acc)
+
+        loop(low // 2, high // 2, body)
 
     def tile4(x):
         return x.reshape(4 * COLS, CH)
@@ -302,8 +304,8 @@
     pick = jnp.where(lax.div(lane, 32) == jnp.where(line < COLS, 0, 3), 1.0, 0.0).astype(BF16)
     decay = sharp[...] * (-1.0 / 256.0)
 
-    for g in range(4):
-        def stretch(b, g=g):
+    def place_group(g):
+        def stretch(b):
             for i in range(8):
                 s = 8 * b + i
                 dx, dy, dz = offset(g * 16 + 4 * b + i // 2)
@@ -317,7 +319,7 @@
 
         for b in range(4):
             at = slice(b * 256, b * 256 + 256)
-            of = slice(g * GROUP + b * 256, g * GROUP + b * 256 + 256)
+            of = aligned(g * GROUP + b * 256, 256, 256)
             wide = dot(tmeta[at, :], spread)
             colb[of, :] = wide[:, 0:128].astype(BF16)
             rowb[of, :] = wide[:, 384:512].astype(BF16)
@@ -328,7 +330,7 @@
             ).astype(BF16)
             w = jnp.exp(radius * decay)
             weight[of, :] = w
-            ew[at, :] = (dot(vals[g * 16 + 4 * b : g * 16 + 4 * b + 4].reshape(256, VALS), embed_w[...]) * w).astype(BF16)
+            ew[at, :] = (dot(vals[pl.ds(g * 16 + 4 * b, 4)].reshape(256, VALS), embed_w[...]) * w).astype(BF16)
 
         both = lax.dot_general(pick, tmeta[...], NT, preferred_element_type=F32)
         colhot[...] = jnp.where(
@@ -345,6 +347,8 @@
                 rows.append((hot * mask[None]).reshape(COLS, GROUP))
             at = slice(b * 512, b * 512 + 512)
             placed[at, :] += dot(jnp.concatenate(rows, axis=0), ew[...])
+
+    loop(0, 4, place_group)
 
     kind = lax.rem(iota((256, CH), 0), 16)
     half_u, half_v = 2 * lax.div(kind, 4) + 1, 2 * lax.rem(kind, 4) + 1
@@ -487,7 +491,7 @@
 
     def keep_gp(rows, acc):
         grad = tile4(gmid[rows]).astype(F32) + acc * tile4(bend[rows])
-        gp[rows.start * COLS : rows.stop * COLS, :] = (
+        gp[aligned(rows.start * COLS, 4 * COLS, 4 * COLS), :] = (
             grad * tile4(inv[rows])
         ).astype(BF16)
 

time: 106 us -> 107 us (level)
  no operation moved by 1% of the time
where the time goes in v4:
time: 107 us
  Pallas kernels  106 us (99%)
    pallas_call x1, Pallas kernels, on_device(): pl.pallas_call(kernel, out_shape=(jax.ShapeDtypeStruct(grid, BF16), jax.S...  101 us
    pallas_call x1, Pallas kernels, on_device(): pl.pallas_call(hand_over, out_shape=(jax.ShapeDtypeStruct(grid, BF16), ja...  4.76 us

profile of v4, /device:TPU:1, one launch (start us, length us, event | category | flops | bytes accessed | tf_op | source)
XLA Modules:
  0.0 106.9 jit_solution(13549759583151099503)
XLA Ops:
  0.6 101.3 %shard_map.111 = (bf16[16,128,256]{2,1,0:T(8,128)(2,1)}, bf16[64,2,32,128]{3,2,1,0:T(8,128)(2,1)}, bf16[2,4608,128]{2,1,0:T(8,128)(2,1)}, f32[128,256]{1,0:T(8,128)}) custom-call(bf16[64,2,32,128]{3,2,1,0:T(8,128)(2,1)} %bitcast.9, s32[32,128]{1,0:T(8,128)} %bitcast.11, s32[32,128]{1,0:T(8,128)} %bitcast.12, s32[1,128]{1,0:T(1,128)} %live_counts.1, ...), custom_call_target="tpu_custom_call" | custom-call | flops 30000001024 | bytes 20000000 | tf_op jit(solution)/shard_map/pallas_call | solution.py:741
  102.0 4.8 %shard_map.112 = (bf16[16,128,256]{2,1,0:T(8,128)(2,1)}, bf16[64,2,32,128]{3,2,1,0:T(8,128)(2,1)}, f32[4608,256]{1,0:T(8,128)}, f32[128,256]{1,0:T(8,128)}) custom-call(bf16[16,128,256]{2,1,0:T(8,128)(2,1)} %get-tuple-element.12.enc_in, bf16[64,2,32,128]{3,2,1,0:T(8,128)(2,1)} %get-tuple-element.13.vg_in, bf16[2,4608,128]{2,1,0:T(8,128)(2,1)} %get-tuple-element.14.grads_in, ...), custom_call_target="tpu_custom_call" | custom-call | tf_op jit(solution)/shard_map/pallas_call | solution.py:768

commit v5 on v3

--- a/solution.py
+++ b/solution.py
@@ -62,7 +62,7 @@
     obs_in, cells, subs, live_counts, sharp, embed_w, conv_in, cot_in,
     enc_out, vg_out, grads_out, embed_out,
     vals, queue, relay, meta_own, meta_z, meta_x, meta, tmeta, colb, rowb, weight, ew, rk, colhot, rowl, placed, counts, inv,
-    cot, conv_w, embed_t, back, bend, base, act_zero, mid, act_one, gmid, gp, act_t, zero_t,
+    cot, conv_w, embed_t, back, bend, pending, base, act_zero, mid, act_one, gmid, gp, act_t, zero_t,
     x3_act, x3_cot, x3_mid, hrow, hcol, strip, stripf,
     vg, grads, total, p0, s1, p1, s2, p2, s3, p3, esum, pe, qe, etotal, enc,
     local_sem, pair_send, pair_recv, a2a_send, a2a_recv, meta_send, meta_recv, vg_send, vg_recv,
@@ -237,25 +237,30 @@
                 spot == COLS - 1, rcorner, pltpu.roll(row, COLS - 1, 0)
             ).astype(BF16)
 
-    def conv(x3, k, finish, flip=False, low=0, high=4):
-        if flip:
-            taps = [
-                conv_w[k, 2 - p, (2 - q) * CH : (3 - q) * CH, :] for p in range(3) for q in range(3)
-            ]
-            taps = jnp.concatenate(taps, axis=1)
-        else:
-            taps = conv_w[k].reshape(9 * CH, CH)
+    def conv(x3, k, finish, flip=False, low=0, high=3):
         for b in range(low, high):
-            near = [x3[4 * b + p : 4 * b + p + 4].reshape(4 * COLS, 3 * CH) for p in range(3)]
-            near = jnp.concatenate(near, axis=1)
+            near = x3[6 * b : 6 * b + 6].reshape(6 * COLS, 3 * CH)
             if flip:
+                taps = [
+                    jnp.concatenate(
+                        [conv_w[k, 2 - p, (2 - q) * CH : (3 - q) * CH, :] for q in range(3)], axis=1
+                    )
+                    for p in range(3)
+                ]
+                taps = jnp.concatenate(taps, axis=0)
                 acc = lax.dot_general(near, taps, NT, preferred_element_type=F32)
             else:
+                taps = jnp.concatenate([conv_w[k, p] for p in range(3)], axis=1)
                 acc = dot(near, taps)
-            finish(slice(4 * b, 4 * b + 4), acc)
-
-    def tile4(x):
-        return x.reshape(4 * COLS, CH)
+            for j in range(6):
+                r = 6 * b + j
+                part = acc[j * COLS : (j + 1) * COLS]
+                if r >= 2:
+                    finish(r - 2, pending[r - 2] + part[:, 2 * CH : 3 * CH])
+                if 1 <= r <= ROWS:
+                    pending[r - 1] += part[:, CH : 2 * CH]
+                if r < ROWS:
+                    pending[r] = part[:, 0:CH]
 
     def grid4(x):
         return x.reshape(4, COLS, CH)
@@ -284,8 +289,8 @@
     embed_t[...] = embed_w[...].T
     halo_finish(cot, 0, x3_cot)
 
-    def keep_back(rows, acc):
-        back[rows] = grid4(acc)
+    def keep_back(r, acc):
+        back[r] = acc
 
     conv(x3_cot, 1, keep_back, flip=True)
     meta_wait(2)
@@ -302,8 +307,8 @@
     pick = jnp.where(lax.div(lane, 32) == jnp.where(line < COLS, 0, 3), 1.0, 0.0).astype(BF16)
     decay = sharp[...] * (-1.0 / 256.0)
 
-    for g in range(4):
-        def stretch(b, g=g):
+    def place_group(g):
+        def stretch(b):
             for i in range(8):
                 s = 8 * b + i
                 dx, dy, dz = offset(g * 16 + 4 * b + i // 2)
@@ -317,7 +322,7 @@
 
         for b in range(4):
             at = slice(b * 256, b * 256 + 256)
-            of = slice(g * GROUP + b * 256, g * GROUP + b * 256 + 256)
+            of = aligned(g * GROUP + b * 256, 256, 256)
             wide = dot(tmeta[at, :], spread)
             colb[of, :] = wide[:, 0:128].astype(BF16)
             rowb[of, :] = wide[:, 384:512].astype(BF16)
@@ -328,7 +333,7 @@
             ).astype(BF16)
             w = jnp.exp(radius * decay)
             weight[of, :] = w
-            ew[at, :] = (dot(vals[g * 16 + 4 * b : g * 16 + 4 * b + 4].reshape(256, VALS), embed_w[...]) * w).astype(BF16)
+            ew[at, :] = (dot(vals[pl.ds(g * 16 + 4 * b, 4)].reshape(256, VALS), embed_w[...]) * w).astype(BF16)
 
         both = lax.dot_general(pick, tmeta[...], NT, preferred_element_type=F32)
         colhot[...] = jnp.where(
@@ -345,6 +350,8 @@
                 rows.append((hot * mask[None]).reshape(COLS, GROUP))
             at = slice(b * 512, b * 512 + 512)
             placed[at, :] += dot(jnp.concatenate(rows, axis=0), ew[...])
+
+    loop(0, 4, place_group)
 
     kind = lax.rem(iota((256, CH), 0), 16)
     half_u, half_v = 2 * lax.div(kind, 4) + 1, 2 * lax.rem(kind, 4) + 1
@@ -374,15 +381,14 @@
     turn_act(act_zero, zero_t)
     halo_finish(act_zero, 1, x3_act)
 
-    def keep_mid(rows, acc):
-        value = (tile4(base[rows]).astype(F32) + acc).astype(BF16)
-        mid[rows] = grid4(value)
+    def keep_mid(r, acc):
+        value = (base[r].astype(F32) + acc).astype(BF16)
+        mid[r] = value
         x = value.astype(F32)
         s = sigmoid(x)
-        act_one[rows] = grid4((x * s).astype(BF16))
+        act_one[r] = (x * s).astype(BF16)
         slope = s * (1.0 + x * (1.0 - s))
-        grad = tile4(cot[rows]).astype(F32) + tile4(back[rows]) * slope
-        gmid[rows] = grid4(grad.astype(BF16))
+        gmid[r] = (cot[r].astype(F32) + back[r] * slope).astype(BF16)
 
     conv(x3_act, 0, keep_mid)
     halo_pack(gmid, 2)
@@ -485,16 +491,14 @@
     kernel_grad(zero_t, x3_mid, 0)
     ar_start(0, 0)
 
-    def keep_gp(rows, acc):
-        grad = tile4(gmid[rows]).astype(F32) + acc * tile4(bend[rows])
-        gp[rows.start * COLS : rows.stop * COLS, :] = (
-            grad * tile4(inv[rows])
-        ).astype(BF16)
+    def keep_gp(r, acc):
+        grad = gmid[r].astype(F32) + acc * bend[r]
+        gp[r * COLS : (r + 1) * COLS, :] = (grad * inv[r]).astype(BF16)
 
     conv(x3_mid, 0, keep_gp, flip=True, low=0, high=2)
     ar_step(1, 1)
     ar_step(0, 0)
-    conv(x3_mid, 0, keep_gp, flip=True, low=2, high=4)
+    conv(x3_mid, 0, keep_gp, flip=True, low=2, high=3)
 
     esum[...] = jnp.zeros_like(esum)
 
@@ -573,8 +577,8 @@
     halo_finish(act_one, 3, x3_act)
     ar_step(1, 5)
 
-    def keep_enc(rows, acc):
-        enc[rows] = grid4((tile4(mid[rows]).astype(F32) + acc).astype(BF16))
+    def keep_enc(r, acc):
+        enc[r] = (mid[r].astype(F32) + acc).astype(BF16)
 
     conv(x3_act, 1, keep_enc, low=0, high=2)
     embed_wait(0)
@@ -587,7 +591,7 @@
     ar_step(0, 5)
     ar_finish(1, 6)
     ar_leave(1).start()
-    conv(x3_act, 1, keep_enc, low=2, high=4)
+    conv(x3_act, 1, keep_enc, low=2, high=3)
     enc_copy = pltpu.make_async_copy(enc, enc_out, local_sem.at[2])
     enc_copy.start()
     embed_wait(1)
@@ -686,6 +690,7 @@
         pltpu.VMEM(grid, BF16),
         pltpu.VMEM((2, 3, 3 * CH, CH), BF16),
         pltpu.VMEM((CH, VALS), BF16),
+        pltpu.VMEM(grid, F32),
         pltpu.VMEM(grid, F32),
         pltpu.VMEM(grid, F32),
         pltpu.VMEM(grid, BF16),

time: 106 us -> 108 us (1.019)
  Pallas kernels: 105 us -> 107 us
    pallas_call x1, Pallas kernels: 101 us -> 103 us  [on_device(): pl.pallas_call(kernel, out_shape=(jax.ShapeDtypeStruct(grid, BF16), jax.S...]
where the time goes in v5:
time: 108 us
  Pallas kernels  107 us (99%)
    pallas_call x1, Pallas kernels, on_device(): pl.pallas_call(kernel, out_shape=(jax.ShapeDtypeStruct(grid, BF16), jax.S...  103 us
    pallas_call x1, Pallas kernels, on_device(): pl.pallas_call(hand_over, out_shape=(jax.ShapeDtypeStruct(grid, BF16), ja...  4.76 us

profile of v5, /device:TPU:1, one launch (start us, length us, event | category | flops | bytes accessed | tf_op | source)
XLA Modules:
  0.0 108.2 jit_solution(9953531781407853383)
XLA Ops:
  0.6 102.6 %shard_map.111 = (bf16[16,128,256]{2,1,0:T(8,128)(2,1)}, bf16[64,2,32,128]{3,2,1,0:T(8,128)(2,1)}, bf16[2,4608,128]{2,1,0:T(8,128)(2,1)}, f32[128,256]{1,0:T(8,128)}) custom-call(bf16[64,2,32,128]{3,2,1,0:T(8,128)(2,1)} %bitcast.9, s32[32,128]{1,0:T(8,128)} %bitcast.11, s32[32,128]{1,0:T(8,128)} %bitcast.12, s32[1,128]{1,0:T(1,128)} %live_counts.1, ...), custom_call_target="tpu_custom_call" | custom-call | flops 30000001024 | bytes 20000000 | tf_op jit(solution)/shard_map/pallas_call | solution.py:742
  103.2 4.8 %shard_map.112 = (bf16[16,128,256]{2,1,0:T(8,128)(2,1)}, bf16[64,2,32,128]{3,2,1,0:T(8,128)(2,1)}, f32[4608,256]{1,0:T(8,128)}, f32[128,256]{1,0:T(8,128)}) custom-call(bf16[16,128,256]{2,1,0:T(8,128)(2,1)} %get-tuple-element.12.enc_in, bf16[64,2,32,128]{3,2,1,0:T(8,128)(2,1)} %get-tuple-element.13.vg_in, bf16[2,4608,128]{2,1,0:T(8,128)(2,1)} %get-tuple-element.14.grads_in, ...), custom_call_target="tpu_custom_call" | custom-call | tf_op jit(solution)/shard_map/pallas_call | solution.py:769

commit v6 on v3

--- a/solution.py
+++ b/solution.py
@@ -63,7 +63,7 @@
     enc_out, vg_out, grads_out, embed_out,
     vals, queue, relay, meta_own, meta_z, meta_x, meta, tmeta, colb, rowb, weight, ew, rk, colhot, rowl, placed, counts, inv,
     cot, conv_w, embed_t, back, bend, base, act_zero, mid, act_one, gmid, gp, act_t, zero_t,
-    x3_act, x3_cot, x3_mid, hrow, hcol, strip, stripf,
+    x3_act, x3_cot, x3_mid, halo, strip, stripf,
     vg, grads, total, p0, s1, p1, s2, p2, s3, p3, esum, pe, qe, etotal, enc,
     local_sem, pair_send, pair_recv, a2a_send, a2a_recv, meta_send, meta_recv, vg_send, vg_recv,
     halo_send, halo_recv, ar_send, ar_recv, em_send, em_recv,
@@ -91,13 +91,22 @@
         obs_in.at[:, 1 - ci], queue.at[:, ci], pair_send.at[0], pair_recv.at[0], lat, other_core
     )
 
-    def greet(j):
-        tlat, tlon = lax.rem(lat + lax.div(j, N_LON), N_LAT), lax.rem(lon + lax.rem(j, N_LON), N_LON)
+    def signal(tlat, tlon):
         pl.semaphore_signal(
             barrier, inc=1, device_id=(tlat, tlon), device_id_type=pl.DeviceIdType.MESH
         )
 
-    loop(1, DEVICES, greet)
+    def greet(j):
+        tx, ty = lax.rem(xi + lax.div(j, 16), 4), lax.rem(yi + lax.rem(j, 4), 4)
+        signal(lax.rem(lat + lax.rem(lax.div(j, 4), 4), 4), tx * 8 + ty * 2 + ci)
+
+    loop(1, 64, greet)
+    beside = lax.rem(lon + N_LON - 1 + 2 * ci, N_LON)
+    for turn in (0, 1, 3):
+        signal(lax.rem(lat + turn, N_LAT), other_core)
+        signal(lax.rem(lat + turn, N_LAT), beside)
+    for d in range(1, 4):
+        signal(lat, xi * 8 + lax.rem(yi + d, 4) * 2 + 1 - ci)
 
     def meta_copies(stage):
         copies = []
@@ -173,18 +182,20 @@
     north, south = lax.rem(lat + 3, N_LAT), lax.rem(lat + 1, N_LAT)
     west, east = lax.rem(lon + N_LON - 1, N_LON), lax.rem(lon + 1, N_LON)
 
+    def halo_row(k, side):
+        return halo.at[k, side * COLS : (side + 1) * COLS]
+
+    def halo_col(k, side, turn):
+        at = 2 * COLS + 16 * (3 * side + turn)
+        return halo.at[k, at : at + 16]
+
     def halo_copies(src, k):
-        pieces = [
-            (src.at[ROWS - 1], hrow.at[k, 0], south, lon),
-            (src.at[0], hrow.at[k, 1], north, lon),
-        ]
+        pieces = [(src.at[ROWS - 1], halo_row(k, 0), south, lon)]
+        pieces.append((src.at[0], halo_row(k, 1), north, lon))
         for side, column, target in ((0, 1, east), (1, 0, west)):
             for turn, tlat in enumerate((lat, south, north)):
-                pieces.append((strip.at[k, column], hcol.at[k, side, turn], tlat, target))
-        return [
-            remote(s, d, halo_send.at[k, i], halo_recv.at[k, i], a, b)
-            for i, (s, d, a, b) in enumerate(pieces)
-        ]
+                pieces.append((strip.at[k, column], halo_col(k, side, turn), tlat, target))
+        return [remote(s, d, halo_send.at[k], halo_recv.at[k], a, b) for s, d, a, b in pieces]
 
     def halo_pack(src, k):
         for r in range(ROWS):
@@ -209,12 +220,12 @@
         loop(low, high, body)
 
     def halo_finish(src, k, x3):
-        for copy in halo_copies(src, k):
-            copy.wait()
+        await_bytes(halo.at[k], halo_recv.at[k])
+        await_bytes(halo.at[k], halo_send.at[k])
         first = iota((16, CH), 0) == 0
         last = iota((16, CH), 0) == 15
-        left = hcol[k, 0, 0].astype(F32)
-        right = hcol[k, 1, 0].astype(F32)
+        left = halo_col(k, 0, 0)[...].astype(F32)
+        right = halo_col(k, 1, 0)[...].astype(F32)
         for r in range(ROWS):
             low = x3[r + 1, 0:16, 0:CH].astype(F32)
             x3[r + 1, 0:16, 0:CH] = jnp.where(first, left[r : r + 1, :], low).astype(BF16)
@@ -228,9 +239,9 @@
             (1, ROWS + 1, 2, 0, lat < N_LAT - 1),
         ):
             keep = jnp.where(valid, 1.0, 0.0).astype(F32)
-            row = hrow[k, side].astype(F32) * keep
-            lcorner = hcol[k, 0, turn].astype(F32)[pick : pick + 1, :] * keep
-            rcorner = hcol[k, 1, turn].astype(F32)[pick : pick + 1, :] * keep
+            row = halo_row(k, side)[...].astype(F32) * keep
+            lcorner = halo_col(k, 0, turn)[...].astype(F32)[pick : pick + 1, :] * keep
+            rcorner = halo_col(k, 1, turn)[...].astype(F32)[pick : pick + 1, :] * keep
             x3[r, :, 0:CH] = jnp.where(spot == 0, lcorner, pltpu.roll(row, 1, 0)).astype(BF16)
             x3[r, :, CH : 2 * CH] = row.astype(BF16)
             x3[r, :, 2 * CH : 3 * CH] = jnp.where(
@@ -266,7 +277,7 @@
 
     cot_copy.wait()
     halo_pack(cot, 0)
-    pl.semaphore_wait(barrier, DEVICES - 1)
+    pl.semaphore_wait(barrier, 72)
     pair_other.start()
     meta_start(0)
     halo_start(cot, 0)
@@ -279,7 +290,7 @@
     pair_own.wait()
     pair_other.wait()
     pltpu.make_async_copy(queue.at[chip], vals.at[0], a2a_recv.at[0]).start()
-    loop(1, 64, send_slot)
+    loop(1, 16, send_slot)
     conv_copy.wait()
     embed_t[...] = embed_w[...].T
     halo_finish(cot, 0, x3_cot)
@@ -287,7 +298,10 @@
     def keep_back(rows, acc):
         back[rows] = grid4(acc)
 
-    conv(x3_cot, 1, keep_back, flip=True)
+    for g in range(1, 4):
+        for j in range(16 * g, 16 * g + 16):
+            send_slot(j)
+        conv(x3_cot, 1, keep_back, flip=True, low=g - 1, high=4 if g == 3 else g)
     meta_wait(2)
 
     placed[...] = jnp.zeros_like(placed)
@@ -412,15 +426,15 @@
         copies = []
         for a, order in enumerate(orders):
             own = a * PART + ci * HALF
-            sems = lambda d: (ar_send.at[k, stage, a, d], ar_recv.at[k, stage, a, d])
+            sems = (ar_send.at[k, stage], ar_recv.at[k, stage])
             quarter = own + coords[order[0]] * QUARTER
             shard = quarter + coords[order[1]] * SHARD
             if stage == 0:
                 src = grads.at[k, aligned(a * PART + (1 - ci) * HALF, HALF, 16)]
-                copies.append(remote(src, p0.at[k, a], *sems(0), lat, other_core))
+                copies.append(remote(src, p0.at[k, a], *sems, lat, other_core))
             elif stage == 6:
                 piece = total.at[k, aligned(own, HALF, 16)]
-                copies.append(remote(piece, piece, *sems(0), lat, other_core))
+                copies.append(remote(piece, piece, *sems, lat, other_core))
             else:
                 axis = order[{1: 0, 2: 1, 3: 2, 4: 1, 5: 0}[stage]]
                 for d in (1, 3, 2):
@@ -437,7 +451,7 @@
                         src = dst = total.at[k, aligned(shard, SHARD, 16)]
                     else:
                         src = dst = total.at[k, aligned(quarter, QUARTER, 16)]
-                    copies.append(remote(src, dst, *sems(d - 1), *along(axis, c)))
+                    copies.append(remote(src, dst, *sems, *along(axis, c)))
         return copies
 
     def ar_start(k, stage):
@@ -445,8 +459,9 @@
             copy.start()
 
     def ar_finish(k, stage):
-        for copy in part_copies(k, stage):
-            copy.wait()
+        amount = (p0, p1, p2, p2, p2, p1, p0)[stage].at[k]
+        await_bytes(amount, ar_recv.at[k, stage])
+        await_bytes(amount, ar_send.at[k, stage])
         for a, order in enumerate(orders):
             own = a * PART + ci * HALF
             if stage == 0:
@@ -557,7 +572,7 @@
                     src, dst = esum.at[aligned(m * 16, 16, 16)], pe.at[d - 1]
                 else:
                     src = dst = etotal.at[aligned(member * 16, 16, 16)]
-            copies.append(remote(src, dst, em_send.at[stage, d - 1], em_recv.at[stage, d - 1], tlat, tlon))
+            copies.append(remote(src, dst, em_send.at[stage], em_recv.at[stage], tlat, tlon))
         return copies
 
     def embed_start(stage):
@@ -565,8 +580,9 @@
             copy.start()
 
     def embed_wait(stage):
-        for copy in embed_copies(stage):
-            copy.wait()
+        amount = qe.at[pl.ds(0, 15)] if stage == 1 else pe
+        await_bytes(amount, em_recv.at[stage])
+        await_bytes(amount, em_send.at[stage])
 
     embed_start(0)
     widen(act_one, x3_act)
@@ -625,17 +641,14 @@
     enc, vg, embed, narrow, wide, in_sem, out_sem,
 ):
     steps = []
-    for i in range(18):
-        src, dst = slice(i % 9 * 2 * CH, (i % 9 + 1) * 2 * CH), slice(i * CH, i * CH + CH)
-        k = i // 9
+    for i in range(6):
+        src, dst = slice(i % 3 * PART, (i % 3 + 1) * PART), slice(i * 3 * CH, (i + 1) * 3 * CH)
+        k = i // 3
         steps.append(
             (grads_in.at[k, src], narrow.at[k, src], wide.at[dst], grads_out.at[dst], (k, src, dst))
         )
-    for i in range(2):
-        at = slice(i * 8, i * 8 + 8)
-        steps.append((enc_in.at[at], enc.at[at], enc.at[at], enc_out.at[at], None))
-        at = slice(i * 32, i * 32 + 32)
-        steps.append((vg_in.at[at], vg.at[at], vg.at[at], vg_out.at[at], None))
+    steps.append((enc_in, enc, enc, enc_out, None))
+    steps.append((vg_in, vg, vg, vg_out, None))
     steps.append((embed_in, embed, embed, embed_out, None))
     moves = [
         pltpu.make_async_copy(step[0], step[1], in_sem.at[i]) for i, step in enumerate(steps)
@@ -647,9 +660,11 @@
         moves[i].wait()
         if at is not None:
             k, rows, to = at
-            for h in range(2):
-                half = slice(rows.start + h * CH, rows.start + h * CH + CH)
-                wide[to, h * 128 : h * 128 + 128] = narrow[k, half, :].astype(F32) * (1.0 / 512.0)
+            for n in range(6):
+                half = slice(rows.start + n * CH, rows.start + n * CH + CH)
+                into = slice(to.start + n // 2 * CH, to.start + (n // 2 + 1) * CH)
+                lanes = slice(n % 2 * 128, n % 2 * 128 + 128)
+                wide[into, lanes] = narrow[k, half, :].astype(F32) * (1.0 / 512.0)
         results.append(pltpu.make_async_copy(src, dst, out_sem.at[i]))
         results[i].start()
     for copy in results:
@@ -699,8 +714,7 @@
         pltpu.VMEM(wide, BF16),
         pltpu.VMEM(wide, BF16),
         pltpu.VMEM(wide, BF16),
-        pltpu.VMEM((4, 2, COLS, CH), BF16),
-        pltpu.VMEM((4, 2, 3, 16, CH), BF16),
+        pltpu.VMEM((4, 2 * COLS + 6 * 16, CH), BF16),
         pltpu.VMEM((4, 2, 16, CH), BF16),
         pltpu.VMEM((2, 16, CH), F32),
         pltpu.VMEM((64, 2, CAP, VALS), BF16),
@@ -727,12 +741,12 @@
         dma((3,)),
         dma,
         dma,
-        dma((4, 8)),
-        dma((4, 8)),
-        dma((2, 7, 3, 3)),
-        dma((2, 7, 3, 3)),
-        dma((3, 15)),
-        dma((3, 15)),
+        dma((4,)),
+        dma((4,)),
+        dma((2, 7)),
+        dma((2, 7)),
+        dma((3,)),
+        dma((3,)),
     ]
     encoded, value_grads, grads, embed_total = pl.pallas_call(
         kernel,
@@ -777,8 +791,8 @@
             pltpu.VMEM((VALS, CH), F32),
             pltpu.VMEM((2, 3 * PART, 128), BF16),
             pltpu.VMEM((3 * PART, CH), F32),
-            dma((23,)),
-            dma((23,)),
+            dma((9,)),
+            dma((9,)),
         ],
         compiler_params=pltpu.CompilerParams(vmem_limit_bytes=60 * 1024 * 1024),
     )(encoded, value_grads, grads, embed_total)

time: 106 us -> 101 us (0.953)
  Pallas kernels: 105 us -> 100 us
    pallas_call x1, Pallas kernels: 101 us -> 96 us  [on_device(): pl.pallas_call(kernel, out_shape=(jax.ShapeDtypeStruct(grid, BF16), jax.S...]
where the time goes in v6:
time: 101 us
  Pallas kernels  100 us (99%)
    pallas_call x1, Pallas kernels, on_device(): pl.pallas_call(kernel, out_shape=(jax.ShapeDtypeStruct(grid, BF16), jax.S...  96 us
    pallas_call x1, Pallas kernels, on_device(): pl.pallas_call(hand_over, out_shape=(jax.ShapeDtypeStruct(grid, BF16), ja...  4.08 us

profile of v6, /device:TPU:1, one launch (start us, length us, event | category | flops | bytes accessed | tf_op | source)
XLA Modules:
  0.0 100.9 jit_solution(16710260650825060223)
XLA Ops:
  0.6 96.0 %shard_map.111 = (bf16[16,128,256]{2,1,0:T(8,128)(2,1)}, bf16[64,2,32,128]{3,2,1,0:T(8,128)(2,1)}, bf16[2,4608,128]{2,1,0:T(8,128)(2,1)}, f32[128,256]{1,0:T(8,128)}) custom-call(bf16[64,2,32,128]{3,2,1,0:T(8,128)(2,1)} %bitcast.9, s32[32,128]{1,0:T(8,128)} %bitcast.11, s32[32,128]{1,0:T(8,128)} %bitcast.12, s32[1,128]{1,0:T(1,128)} %live_counts.1, ...), custom_call_target="tpu_custom_call" | custom-call | flops 30000001024 | bytes 20000000 | tf_op jit(solution)/shard_map/pallas_call | solution.py:751
  96.6 4.1 %shard_map.112 = (bf16[16,128,256]{2,1,0:T(8,128)(2,1)}, bf16[64,2,32,128]{3,2,1,0:T(8,128)(2,1)}, f32[4608,256]{1,0:T(8,128)}, f32[128,256]{1,0:T(8,128)}) custom-call(bf16[16,128,256]{2,1,0:T(8,128)(2,1)} %get-tuple-element.12.enc_in, bf16[64,2,32,128]{3,2,1,0:T(8,128)(2,1)} %get-tuple-element.13.vg_in, bf16[2,4608,128]{2,1,0:T(8,128)(2,1)} %get-tuple-element.14.grads_in, ...), custom_call_target="tpu_custom_call" | custom-call | tf_op jit(solution)/shard_map/pallas_call | solution.py:778

commit v7 on v6

--- a/solution.py
+++ b/solution.py
@@ -77,9 +77,17 @@
     yc = lax.rem(lon, 8)
     other_core = lon + 1 - 2 * ci
 
+    to_x = [xi] + [lax.rem(xi + d, 4) for d in range(1, 4)]
+    to_y = [yi] + [lax.rem(yi + d, 4) for d in range(1, 4)]
+    to_z = [lat] + [lax.rem(lat + d, 4) for d in range(1, 4)]
+
     def offset(j):
-        g, dx, dy = lax.div(j, 16), lax.rem(lax.div(j, 4), 4), lax.rem(j, 4)
-        return dx, dy, lax.rem(g + 8 - dx - dy, 4)
+        dx, dy = j // 4 % 4, j % 4
+        return dx, dy, (j // 16 + 8 - dx - dy) % 4
+
+    def source(j):
+        dx, dy, dz = offset(j)
+        return to_x[-dx % 4], to_y[-dy % 4], to_z[-dz % 4]
 
     barrier = pltpu.get_barrier_semaphore()
 
@@ -96,17 +104,14 @@
             barrier, inc=1, device_id=(tlat, tlon), device_id_type=pl.DeviceIdType.MESH
         )
 
-    def greet(j):
-        tx, ty = lax.rem(xi + lax.div(j, 16), 4), lax.rem(yi + lax.rem(j, 4), 4)
-        signal(lax.rem(lat + lax.rem(lax.div(j, 4), 4), 4), tx * 8 + ty * 2 + ci)
-
-    loop(1, 64, greet)
+    for j in range(1, 64):
+        signal(to_z[j // 4 % 4], to_x[j // 16] * 8 + to_y[j % 4] * 2 + ci)
     beside = lax.rem(lon + N_LON - 1 + 2 * ci, N_LON)
     for turn in (0, 1, 3):
-        signal(lax.rem(lat + turn, N_LAT), other_core)
-        signal(lax.rem(lat + turn, N_LAT), beside)
+        signal(to_z[turn], other_core)
+        signal(to_z[turn], beside)
     for d in range(1, 4):
-        signal(lat, xi * 8 + lax.rem(yi + d, 4) * 2 + 1 - ci)
+        signal(lat, xi * 8 + to_y[d] * 2 + 1 - ci)
 
     def meta_copies(stage):
         copies = []
@@ -172,8 +177,8 @@
 
     def send_slot(j):
         dx, dy, dz = offset(j)
-        tx, ty, tz = lax.rem(xi + dx, 4), lax.rem(yi + dy, 4), lax.rem(lat + dz, 4)
-        g = lax.div(j, 16)
+        tx, ty, tz = to_x[dx], to_y[dy], to_z[dz]
+        g = j // 16
         remote(
             queue.at[tz * 16 + tx * 4 + ty], vals.at[j], a2a_send.at[g], a2a_recv.at[g],
             tz, tx * 8 + ty * 2 + ci,
@@ -290,7 +295,8 @@
     pair_own.wait()
     pair_other.wait()
     pltpu.make_async_copy(queue.at[chip], vals.at[0], a2a_recv.at[0]).start()
-    loop(1, 16, send_slot)
+    for j in range(1, 16):
+        send_slot(j)
     conv_copy.wait()
     embed_t[...] = embed_w[...].T
     halo_finish(cot, 0, x3_cot)
@@ -317,16 +323,10 @@
     decay = sharp[...] * (-1.0 / 256.0)
 
     for g in range(4):
-        def stretch(b, g=g):
-            for i in range(8):
-                s = 8 * b + i
-                dx, dy, dz = offset(g * 16 + 4 * b + i // 2)
-                sx, sy = lax.rem(xi + 4 - dx, 4), lax.rem(yi + 4 - dy, 4)
-                source = meta[sy * 2 + i % 2, sx, lax.rem(lat + 4 - dz, 4)]
-                line = jnp.broadcast_to(source, (CAP, 128)) * slot_mask
-                tmeta[aligned(s * CAP, CAP, CAP), :] = line.astype(BF16)
-
-        loop(0, 4, stretch)
+        for s in range(32):
+            sx, sy, sz = source(g * 16 + s // 2)
+            line = jnp.broadcast_to(meta[sy * 2 + s % 2, sx, sz], (CAP, 128)) * slot_mask
+            tmeta[s * CAP : s * CAP + CAP, :] = line.astype(BF16)
         await_bytes(vals.at[pl.ds(g * 16, 16)], a2a_recv.at[g])
 
         for b in range(4):
@@ -409,8 +409,11 @@
             block = dot(act_t[...], x3[2 - p : 2 - p + ROWS].reshape(CELLS, 3 * CH))
             for q in range(3):
                 for h in range(2):
-                    at, lanes = (6 * p + 2 * q + h) * CH, (2 - q) * CH + h * 128
-                    grads[k, at : at + CH, :] = block[:, lanes : lanes + 128].astype(BF16)
+                    n, lanes = 6 * p + 2 * q + h, (2 - q) * CH + h * 128
+                    at = n % 3 * CH
+                    grads[k, n // 6, n // 3 % 2, at : at + CH, :] = block[
+                        :, lanes : lanes + 128
+                    ].astype(BF16)
 
     coords = {"x": xi, "y": yi, "z": lat}
     orders = (("x", "y", "z"), ("y", "z", "x"), ("z", "x", "y"))
@@ -420,38 +423,33 @@
         return cz, cx * 8 + cy * 2 + ci
 
     def turned(axis, d):
-        return lax.rem(coords[axis] + d, 4)
+        return {"x": to_x, "y": to_y, "z": to_z}[axis][d]
 
     def part_copies(k, stage):
+        sems = (ar_send.at[k, stage], ar_recv.at[k, stage])
+        if stage == 0:
+            return [remote(grads.at[k, :, 1 - ci], p0.at[k], *sems, lat, other_core)]
+        if stage == 6:
+            half = total.at[k, :, ci]
+            return [remote(half, half, *sems, lat, other_core)]
         copies = []
         for a, order in enumerate(orders):
-            own = a * PART + ci * HALF
-            sems = (ar_send.at[k, stage], ar_recv.at[k, stage])
-            quarter = own + coords[order[0]] * QUARTER
+            quarter = coords[order[0]] * QUARTER
             shard = quarter + coords[order[1]] * SHARD
-            if stage == 0:
-                src = grads.at[k, aligned(a * PART + (1 - ci) * HALF, HALF, 16)]
-                copies.append(remote(src, p0.at[k, a], *sems, lat, other_core))
-            elif stage == 6:
-                piece = total.at[k, aligned(own, HALF, 16)]
-                copies.append(remote(piece, piece, *sems, lat, other_core))
-            else:
-                axis = order[{1: 0, 2: 1, 3: 2, 4: 1, 5: 0}[stage]]
-                for d in (1, 3, 2):
-                    c = turned(axis, d)
-                    if stage == 1:
-                        src = s1.at[k, a, aligned(c * QUARTER, QUARTER, 16)]
-                        dst = p1.at[k, a, d - 1]
-                    elif stage == 2:
-                        src = s2.at[k, a, aligned(c * SHARD, SHARD, 16)]
-                        dst = p2.at[k, a, d - 1]
-                    elif stage == 3:
-                        src, dst = s3.at[k, a], p3.at[k, a, coords[axis]]
-                    elif stage == 4:
-                        src = dst = total.at[k, aligned(shard, SHARD, 16)]
-                    else:
-                        src = dst = total.at[k, aligned(quarter, QUARTER, 16)]
-                    copies.append(remote(src, dst, *sems, *along(axis, c)))
+            axis = order[{1: 0, 2: 1, 3: 2, 4: 1, 5: 0}[stage]]
+            for d in (1, 3, 2):
+                c = turned(axis, d)
+                if stage == 1:
+                    src, dst = s1.at[k, a, aligned(c * QUARTER, QUARTER, 16)], p1.at[k, a, d - 1]
+                elif stage == 2:
+                    src, dst = s2.at[k, a, aligned(c * SHARD, SHARD, 16)], p2.at[k, a, d - 1]
+                elif stage == 3:
+                    src, dst = s3.at[k, a], p3.at[k, a, coords[axis]]
+                elif stage == 4:
+                    src = dst = total.at[k, a, ci, aligned(shard, SHARD, 16)]
+                else:
+                    src = dst = total.at[k, a, ci, aligned(quarter, QUARTER, 16)]
+                copies.append(remote(src, dst, *sems, *along(axis, c)))
         return copies
 
     def ar_start(k, stage):
@@ -463,9 +461,8 @@
         await_bytes(amount, ar_recv.at[k, stage])
         await_bytes(amount, ar_send.at[k, stage])
         for a, order in enumerate(orders):
-            own = a * PART + ci * HALF
             if stage == 0:
-                here = grads[k, aligned(own, HALF, 16), :].astype(F32)
+                here = grads[k, a, ci].astype(F32)
                 s1[k, a] = (here + p0[k, a].astype(F32)).astype(BF16)
             elif stage in (1, 2):
                 size = QUARTER if stage == 1 else SHARD
@@ -480,9 +477,9 @@
                 whole = p3[k, a, 0].astype(F32)
                 for d in range(1, 4):
                     whole += p3[k, a, d].astype(F32)
-                quarter = own + coords[order[0]] * QUARTER
+                quarter = coords[order[0]] * QUARTER
                 at = aligned(quarter + coords[order[1]] * SHARD, SHARD, 16)
-                total[k, at, :] = whole.astype(BF16)
+                total[k, a, ci, at, :] = whole.astype(BF16)
 
     def ar_step(k, stage):
         ar_finish(k, stage)
@@ -514,8 +511,7 @@
     esum[...] = jnp.zeros_like(esum)
 
     def vg_copy(j):
-        dx, dy, dz = offset(j)
-        sx, sy, sz = lax.rem(xi + 4 - dx, 4), lax.rem(yi + 4 - dy, 4), lax.rem(lat + 4 - dz, 4)
+        sx, sy, sz = source(j)
         return remote(vg.at[j], relay.at[chip], vg_send, vg_recv, sz, sx * 8 + sy * 2 + ci)
 
     def gather(b):
@@ -587,12 +583,12 @@
     embed_start(0)
     widen(act_one, x3_act)
     halo_finish(act_one, 3, x3_act)
-    ar_step(1, 5)
 
     def keep_enc(rows, acc):
         enc[rows] = grid4((tile4(mid[rows]).astype(F32) + acc).astype(BF16))
 
-    conv(x3_act, 1, keep_enc, low=0, high=2)
+    conv(x3_act, 1, keep_enc, low=0, high=1)
+    ar_step(1, 5)
     embed_wait(0)
     own_rows = aligned(member * 16, 16, 16)
     mine = esum[own_rows, :]
@@ -600,12 +596,11 @@
         mine += pe[d]
     esum[own_rows, :] = mine
     embed_start(1)
+    conv(x3_act, 1, keep_enc, low=1, high=2)
     ar_step(0, 5)
+    conv(x3_act, 1, keep_enc, low=2, high=3)
     ar_finish(1, 6)
     ar_leave(1).start()
-    conv(x3_act, 1, keep_enc, low=2, high=4)
-    enc_copy = pltpu.make_async_copy(enc, enc_out, local_sem.at[2])
-    enc_copy.start()
     embed_wait(1)
     qe[column] = esum[own_rows, :]
     whole = qe[0]
@@ -620,6 +615,9 @@
         relay.at[:, 1 - ci], vg_out.at[:, ci], pair_send.at[1], pair_recv.at[1], lat, other_core
     )
     vg_other.start()
+    conv(x3_act, 1, keep_enc, low=3, high=4)
+    enc_copy = pltpu.make_async_copy(enc, enc_out, local_sem.at[2])
+    enc_copy.start()
     ar_finish(0, 6)
     ar_leave(0).start()
     embed_wait(2)
@@ -718,8 +716,8 @@
         pltpu.VMEM((4, 2, 16, CH), BF16),
         pltpu.VMEM((2, 16, CH), F32),
         pltpu.VMEM((64, 2, CAP, VALS), BF16),
-        pltpu.VMEM((2, 3 * PART, 128), BF16),
-        pltpu.VMEM((2, 3 * PART, 128), BF16),
+        pltpu.VMEM((2, 3, 2, HALF, 128), BF16),
+        pltpu.VMEM((2, 3, 2, HALF, 128), BF16),
         pltpu.VMEM((2, 3, HALF, 128), BF16),
         pltpu.VMEM((2, 3, HALF, 128), BF16),
         pltpu.VMEM((2, 3, 3, QUARTER, 128), BF16),
@@ -753,7 +751,7 @@
         out_shape=(
             jax.ShapeDtypeStruct(grid, BF16),
             jax.ShapeDtypeStruct((64, 2, CAP, VALS), BF16),
-            jax.ShapeDtypeStruct((2, 3 * PART, 128), BF16),
+            jax.ShapeDtypeStruct((2, 3, 2, HALF, 128), BF16),
             jax.ShapeDtypeStruct((VALS, CH), F32),
         ),
         in_specs=[anywhere, vmem, vmem, vmem, vmem, vmem, anywhere, anywhere],
@@ -795,7 +793,7 @@
             dma((9,)),
         ],
         compiler_params=pltpu.CompilerParams(vmem_limit_bytes=60 * 1024 * 1024),
-    )(encoded, value_grads, grads, embed_total)
+    )(encoded, value_grads, grads.reshape(2, 3 * PART, 128), embed_total)
     return (
         encoded,
         value_grads.reshape(OBS, VALS),

time: 101 us -> 99.9 us (0.989)
  Pallas kernels: 100 us -> 98.9 us
    pallas_call x1, Pallas kernels: 96 us -> 94.8 us  [on_device(): pl.pallas_call(kernel, out_shape=(jax.ShapeDtypeStruct(grid, BF16), jax.S...]
where the time goes in v7:
time: 99.9 us; the launch traced here: 99.7 us
  Pallas kernels  98.9 us (99%)
    pallas_call x1, Pallas kernels, on_device(): pl.pallas_call(kernel, out_shape=(jax.ShapeDtypeStruct(grid, BF16), jax.S...  94.8 us
    pallas_call x1, Pallas kernels, on_device(): pl.pallas_call(hand_over, out_shape=(jax.ShapeDtypeStruct(grid, BF16), ja...  4.08 us

profile of v7, /device:TPU:1, one launch (start us, length us, event | category | flops | bytes accessed | tf_op | source)
XLA Modules:
  0.0 99.7 jit_solution(5425031153957932511)
XLA Ops:
  0.6 94.8 %shard_map.111 = (bf16[16,128,256]{2,1,0:T(8,128)(2,1)}, bf16[64,2,32,128]{3,2,1,0:T(8,128)(2,1)}, bf16[2,3,2,768,128]{4,3,2,1,0:T(8,128)(2,1)}, f32[128,256]{1,0:T(8,128)}) custom-call(bf16[64,2,32,128]{3,2,1,0:T(8,128)(2,1)} %bitcast.11, s32[32,128]{1,0:T(8,128)} %bitcast.13, s32[32,128]{1,0:T(8,128)} %bitcast.14, s32[1,128]{1,0:T(1,128)} %live_counts.1, ...), custom_call_target="tpu_custom_call" | custom-call | flops 30000001024 | bytes 20000000 | tf_op jit(solution)/shard_map/pallas_call | solution.py:749
  95.4 4.1 %shard_map.112 = (bf16[16,128,256]{2,1,0:T(8,128)(2,1)}, bf16[64,2,32,128]{3,2,1,0:T(8,128)(2,1)}, f32[4608,256]{1,0:T(8,128)}, f32[128,256]{1,0:T(8,128)}) custom-call(bf16[16,128,256]{2,1,0:T(8,128)(2,1)} %get-tuple-element.12.enc_in, bf16[64,2,32,128]{3,2,1,0:T(8,128)(2,1)} %get-tuple-element.13.vg_in, bf16[2,4608,128]{2,1,0:T(8,128)(2,1)} %bitcast.8, ...), custom_call_target="tpu_custom_call" | custom-call | tf_op jit(solution)/shard_map/pallas_call | solution.py:776

commit v8 on v7

--- a/solution.py
+++ b/solution.py
@@ -146,32 +146,6 @@
     def meta_sent(stage):
         await_bytes((meta_z, meta_x, meta)[stage].at[pl.ds(0, (3, 3, 7)[stage])], meta_send.at[stage])
 
-    line, lane = iota((32, 128), 0), iota((32, 128), 1)
-    own_four = jnp.where(lax.div(lane, 4) == line, live_counts[...].astype(F32), 0.0).astype(BF16)
-    to_slots = jnp.where(
-        lax.rem(iota((128, 128), 0), 4) == lax.div(iota((128, 128), 1), 32), 1.0, 0.0
-    ).astype(BF16)
-    live = lax.rem(lane, 32).astype(F32) < dot(own_four, to_slots)
-    cell, sub = cells[...], subs[...]
-    u, v = sub >> 3, sub & 7
-    u = jnp.where(u >= 4, u - 4, 3 - u)
-    v = jnp.where(v >= 4, v - 4, 3 - v)
-    row = cell >> 7
-    fields = [
-        jnp.where(live, (cell & 127).astype(F32), 255.0),
-        (row * 16 + u * 4 + v).astype(F32),
-        ((2 * u + 1) * (2 * u + 1) + (2 * v + 1) * (2 * v + 1)).astype(F32),
-        row.astype(F32),
-    ]
-    for i in range(4):
-        mixed = jnp.zeros((32, 128), F32)
-        for f in range(4):
-            shift = (f - i) * 32 % 128
-            turned_field = pltpu.roll(fields[f], shift, 1) if shift else fields[f]
-            mixed = jnp.where(lax.div(lane, 32) == f, turned_field, mixed)
-        for r in range(32):
-            meta_own[i, r] = mixed[r : r + 1, :]
-
     conv_copy = pltpu.make_async_copy(conv_in, conv_w, local_sem.at[1])
     conv_copy.start()
 
@@ -213,16 +187,12 @@
         for copy in halo_copies(src, k):
             copy.start()
 
-    def widen(src, x3, low=0, high=4):
-        def body(b):
-            for i in range(4):
-                r = 4 * b + i
-                row = src[r].astype(F32)
-                x3[r + 1, :, 0:CH] = pltpu.roll(row, 1, 0).astype(BF16)
-                x3[r + 1, :, CH : 2 * CH] = src[r]
-                x3[r + 1, :, 2 * CH : 3 * CH] = pltpu.roll(row, COLS - 1, 0).astype(BF16)
-
-        loop(low, high, body)
+    def widen(src, x3, low=0, high=ROWS):
+        for r in range(low, high):
+            row = src[r].astype(F32)
+            x3[r + 1, :, 0:CH] = pltpu.roll(row, 1, 0).astype(BF16)
+            x3[r + 1, :, CH : 2 * CH] = src[r]
+            x3[r + 1, :, 2 * CH : 3 * CH] = pltpu.roll(row, COLS - 1, 0).astype(BF16)
 
     def halo_finish(src, k, x3):
         await_bytes(halo.at[k], halo_recv.at[k])
@@ -280,16 +250,44 @@
         for r in range(ROWS):
             act_t[:, r * COLS : (r + 1) * COLS] = act[r].T
 
+    def own_meta():
+        line, lane = iota((32, 128), 0), iota((32, 128), 1)
+        own_four = jnp.where(lax.div(lane, 4) == line, live_counts[...].astype(F32), 0.0).astype(BF16)
+        to_slots = jnp.where(
+            lax.rem(iota((128, 128), 0), 4) == lax.div(iota((128, 128), 1), 32), 1.0, 0.0
+        ).astype(BF16)
+        live = lax.rem(lane, 32).astype(F32) < dot(own_four, to_slots)
+        cell, sub = cells[...], subs[...]
+        u, v = sub >> 3, sub & 7
+        u = jnp.where(u >= 4, u - 4, 3 - u)
+        v = jnp.where(v >= 4, v - 4, 3 - v)
+        row = cell >> 7
+        fields = [
+            jnp.where(live, (cell & 127).astype(F32), 255.0),
+            (row * 16 + u * 4 + v).astype(F32),
+            ((2 * u + 1) * (2 * u + 1) + (2 * v + 1) * (2 * v + 1)).astype(F32),
+            row.astype(F32),
+        ]
+        for i in range(4):
+            mixed = jnp.zeros((32, 128), F32)
+            for f in range(4):
+                shift = (f - i) * 32 % 128
+                turned_field = pltpu.roll(fields[f], shift, 1) if shift else fields[f]
+                mixed = jnp.where(lax.div(lane, 32) == f, turned_field, mixed)
+            for r in range(32):
+                meta_own[i, r] = mixed[r : r + 1, :]
+
+    pl.semaphore_wait(barrier, 72)
+    pair_other.start()
+    own_meta()
+    meta_start(0)
     cot_copy.wait()
     halo_pack(cot, 0)
-    pl.semaphore_wait(barrier, 72)
-    pair_other.start()
-    meta_start(0)
     halo_start(cot, 0)
-    widen(cot, x3_cot, 0, 2)
+    widen(cot, x3_cot, 0, 8)
     meta_wait(0)
     meta_start(1)
-    widen(cot, x3_cot, 2, 4)
+    widen(cot, x3_cot, 8, 16)
     meta_wait(1)
     meta_start(2)
     pair_own.wait()
@@ -404,8 +402,10 @@
     halo_pack(act_one, 3)
     halo_start(act_one, 3)
 
-    def kernel_grad(act_t, x3, k):
+    def kernel_grad(act_t, x3, k, beside=None):
         for p in range(3):
+            if beside is not None:
+                beside(p)
             block = dot(act_t[...], x3[2 - p : 2 - p + ROWS].reshape(CELLS, 3 * CH))
             for q in range(3):
                 for h in range(2):
@@ -489,9 +489,8 @@
         return pltpu.make_async_copy(total.at[k], grads_out.at[k], local_sem.at[3 if k else 6])
 
     turn_act(act_one, act_t)
-    kernel_grad(act_t, x3_cot, 1)
+    kernel_grad(act_t, x3_cot, 1, lambda p: widen(gmid, x3_mid, (0, 6, 11)[p], (6, 11, 16)[p]))
     ar_start(1, 0)
-    widen(gmid, x3_mid)
     halo_finish(gmid, 2, x3_mid)
     ar_step(1, 0)
     kernel_grad(zero_t, x3_mid, 0)
@@ -515,6 +514,7 @@
         return remote(vg.at[j], relay.at[chip], vg_send, vg_recv, sz, sx * 8 + sy * 2 + ci)
 
     def gather(b):
+        widen(act_one, x3_act, 2 * b, 2 * b + 2)
         at = slice(b * 512, b * 512 + 512)
         chips = slice(b * 8, b * 8 + 8)
         hot = jnp.where(
@@ -581,7 +581,6 @@
         await_bytes(amount, em_send.at[stage])
 
     embed_start(0)
-    widen(act_one, x3_act)
     halo_finish(act_one, 3, x3_act)
 
     def keep_enc(rows, acc):

time: 99.9 us -> 101 us (1.011)
  Pallas kernels: 98.9 us -> 100 us
    pallas_call x1, Pallas kernels: 94.8 us -> 96 us  [on_device(): pl.pallas_call(kernel, out_shape=(jax.ShapeDtypeStruct(grid, BF16), jax.S...]
where the time goes in v8:
time: 101 us
  Pallas kernels  100 us (99%)
    pallas_call x1, Pallas kernels, on_device(): pl.pallas_call(kernel, out_shape=(jax.ShapeDtypeStruct(grid, BF16), jax.S...  96 us
    pallas_call x1, Pallas kernels, on_device(): pl.pallas_call(hand_over, out_shape=(jax.ShapeDtypeStruct(grid, BF16), ja...  4.08 us

profile of v8, /device:TPU:1, one launch (start us, length us, event | category | flops | bytes accessed | tf_op | source)
XLA Modules:
  0.0 100.9 jit_solution(9365519540888909547)
XLA Ops:
  0.6 96.0 %shard_map.111 = (bf16[16,128,256]{2,1,0:T(8,128)(2,1)}, bf16[64,2,32,128]{3,2,1,0:T(8,128)(2,1)}, bf16[2,3,2,768,128]{4,3,2,1,0:T(8,128)(2,1)}, f32[128,256]{1,0:T(8,128)}) custom-call(bf16[64,2,32,128]{3,2,1,0:T(8,128)(2,1)} %bitcast.11, s32[32,128]{1,0:T(8,128)} %bitcast.13, s32[32,128]{1,0:T(8,128)} %bitcast.14, s32[1,128]{1,0:T(1,128)} %live_counts.1, ...), custom_call_target="tpu_custom_call" | custom-call | flops 30000001024 | bytes 20000000 | tf_op jit(solution)/shard_map/pallas_call | solution.py:748
  96.6 4.1 %shard_map.112 = (bf16[16,128,256]{2,1,0:T(8,128)(2,1)}, bf16[64,2,32,128]{3,2,1,0:T(8,128)(2,1)}, f32[4608,256]{1,0:T(8,128)}, f32[128,256]{1,0:T(8,128)}) custom-call(bf16[16,128,256]{2,1,0:T(8,128)(2,1)} %get-tuple-element.12.enc_in, bf16[64,2,32,128]{3,2,1,0:T(8,128)(2,1)} %get-tuple-element.13.vg_in, bf16[2,4608,128]{2,1,0:T(8,128)(2,1)} %bitcast.8, ...), custom_call_target="tpu_custom_call" | custom-call | tf_op jit(solution)/shard_map/pallas_call | solution.py:775

commit v9 on v7

--- a/solution.py
+++ b/solution.py
@@ -286,17 +286,19 @@
     pair_other.start()
     meta_start(0)
     halo_start(cot, 0)
-    widen(cot, x3_cot, 0, 2)
     meta_wait(0)
     meta_start(1)
-    widen(cot, x3_cot, 2, 4)
-    meta_wait(1)
-    meta_start(2)
+    widen(cot, x3_cot, 0, 2)
     pair_own.wait()
     pair_other.wait()
     pltpu.make_async_copy(queue.at[chip], vals.at[0], a2a_recv.at[0]).start()
     for j in range(1, 16):
         send_slot(j)
+    meta_wait(1)
+    meta_start(2)
+    for j in range(16, 32):
+        send_slot(j)
+    widen(cot, x3_cot, 2, 4)
     conv_copy.wait()
     embed_t[...] = embed_w[...].T
     halo_finish(cot, 0, x3_cot)
@@ -304,10 +306,10 @@
     def keep_back(rows, acc):
         back[rows] = grid4(acc)
 
-    for g in range(1, 4):
+    for g in range(2, 4):
         for j in range(16 * g, 16 * g + 16):
             send_slot(j)
-        conv(x3_cot, 1, keep_back, flip=True, low=g - 1, high=4 if g == 3 else g)
+        conv(x3_cot, 1, keep_back, flip=True, low=2 * g - 4, high=2 * g - 2)
     meta_wait(2)
 
     placed[...] = jnp.zeros_like(placed)

time: 99.9 us -> 97.8 us (0.979)
  Pallas kernels: 98.9 us -> 96.8 us
    pallas_call x1, Pallas kernels: 94.8 us -> 92.7 us  [on_device(): pl.pallas_call(kernel, out_shape=(jax.ShapeDtypeStruct(grid, BF16), jax.S...]
where the time goes in v9:
time: 97.8 us; the launch traced here: 97.6 us
  Pallas kernels  96.8 us (99%)
    pallas_call x1, Pallas kernels, on_device(): pl.pallas_call(kernel, out_shape=(jax.ShapeDtypeStruct(grid, BF16), jax.S...  92.7 us
    pallas_call x1, Pallas kernels, on_device(): pl.pallas_call(hand_over, out_shape=(jax.ShapeDtypeStruct(grid, BF16), ja...  4.08 us

profile of v9, /device:TPU:1, one launch (start us, length us, event | category | flops | bytes accessed | tf_op | source)
XLA Modules:
  0.0 97.6 jit_solution(1459367429674517007)
XLA Ops:
  0.6 92.7 %shard_map.111 = (bf16[16,128,256]{2,1,0:T(8,128)(2,1)}, bf16[64,2,32,128]{3,2,1,0:T(8,128)(2,1)}, bf16[2,3,2,768,128]{4,3,2,1,0:T(8,128)(2,1)}, f32[128,256]{1,0:T(8,128)}) custom-call(bf16[64,2,32,128]{3,2,1,0:T(8,128)(2,1)} %bitcast.11, s32[32,128]{1,0:T(8,128)} %bitcast.13, s32[32,128]{1,0:T(8,128)} %bitcast.14, s32[1,128]{1,0:T(1,128)} %live_counts.1, ...), custom_call_target="tpu_custom_call" | custom-call | flops 30000001024 | bytes 20000000 | tf_op jit(solution)/shard_map/pallas_call | solution.py:751
  93.3 4.1 %shard_map.112 = (bf16[16,128,256]{2,1,0:T(8,128)(2,1)}, bf16[64,2,32,128]{3,2,1,0:T(8,128)(2,1)}, f32[4608,256]{1,0:T(8,128)}, f32[128,256]{1,0:T(8,128)}) custom-call(bf16[16,128,256]{2,1,0:T(8,128)(2,1)} %get-tuple-element.12.enc_in, bf16[64,2,32,128]{3,2,1,0:T(8,128)(2,1)} %get-tuple-element.13.vg_in, bf16[2,4608,128]{2,1,0:T(8,128)(2,1)} %bitcast.8, ...), custom_call_target="tpu_custom_call" | custom-call | tf_op jit(solution)/shard_map/pallas_call | solution.py:778

commit v10 on v8

--- a/solution.py
+++ b/solution.py
@@ -187,12 +187,16 @@
         for copy in halo_copies(src, k):
             copy.start()
 
-    def widen(src, x3, low=0, high=ROWS):
-        for r in range(low, high):
-            row = src[r].astype(F32)
-            x3[r + 1, :, 0:CH] = pltpu.roll(row, 1, 0).astype(BF16)
-            x3[r + 1, :, CH : 2 * CH] = src[r]
-            x3[r + 1, :, 2 * CH : 3 * CH] = pltpu.roll(row, COLS - 1, 0).astype(BF16)
+    def widen(src, x3, low=0, high=4):
+        def body(b):
+            for i in range(4):
+                r = 4 * b + i
+                row = src[r].astype(F32)
+                x3[r + 1, :, 0:CH] = pltpu.roll(row, 1, 0).astype(BF16)
+                x3[r + 1, :, CH : 2 * CH] = src[r]
+                x3[r + 1, :, 2 * CH : 3 * CH] = pltpu.roll(row, COLS - 1, 0).astype(BF16)
+
+        loop(low, high, body)
 
     def halo_finish(src, k, x3):
         await_bytes(halo.at[k], halo_recv.at[k])
@@ -284,17 +288,19 @@
     cot_copy.wait()
     halo_pack(cot, 0)
     halo_start(cot, 0)
-    widen(cot, x3_cot, 0, 8)
     meta_wait(0)
     meta_start(1)
-    widen(cot, x3_cot, 8, 16)
-    meta_wait(1)
-    meta_start(2)
+    widen(cot, x3_cot, 0, 2)
     pair_own.wait()
     pair_other.wait()
     pltpu.make_async_copy(queue.at[chip], vals.at[0], a2a_recv.at[0]).start()
     for j in range(1, 16):
         send_slot(j)
+    meta_wait(1)
+    meta_start(2)
+    for j in range(16, 64):
+        send_slot(j)
+    widen(cot, x3_cot, 2, 4)
     conv_copy.wait()
     embed_t[...] = embed_w[...].T
     halo_finish(cot, 0, x3_cot)
@@ -302,10 +308,7 @@
     def keep_back(rows, acc):
         back[rows] = grid4(acc)
 
-    for g in range(1, 4):
-        for j in range(16 * g, 16 * g + 16):
-            send_slot(j)
-        conv(x3_cot, 1, keep_back, flip=True, low=g - 1, high=4 if g == 3 else g)
+    conv(x3_cot, 1, keep_back, flip=True)
     meta_wait(2)
 
     placed[...] = jnp.zeros_like(placed)
@@ -402,10 +405,8 @@
     halo_pack(act_one, 3)
     halo_start(act_one, 3)
 
-    def kernel_grad(act_t, x3, k, beside=None):
+    def kernel_grad(act_t, x3, k):
         for p in range(3):
-            if beside is not None:
-                beside(p)
             block = dot(act_t[...], x3[2 - p : 2 - p + ROWS].reshape(CELLS, 3 * CH))
             for q in range(3):
                 for h in range(2):
@@ -489,8 +490,9 @@
         return pltpu.make_async_copy(total.at[k], grads_out.at[k], local_sem.at[3 if k else 6])
 
     turn_act(act_one, act_t)
-    kernel_grad(act_t, x3_cot, 1, lambda p: widen(gmid, x3_mid, (0, 6, 11)[p], (6, 11, 16)[p]))
+    kernel_grad(act_t, x3_cot, 1)
     ar_start(1, 0)
+    widen(gmid, x3_mid)
     halo_finish(gmid, 2, x3_mid)
     ar_step(1, 0)
     kernel_grad(zero_t, x3_mid, 0)
@@ -514,7 +516,6 @@
         return remote(vg.at[j], relay.at[chip], vg_send, vg_recv, sz, sx * 8 + sy * 2 + ci)
 
     def gather(b):
-        widen(act_one, x3_act, 2 * b, 2 * b + 2)
         at = slice(b * 512, b * 512 + 512)
         chips = slice(b * 8, b * 8 + 8)
         hot = jnp.where(
@@ -581,6 +582,7 @@
         await_bytes(amount, em_send.at[stage])
 
     embed_start(0)
+    widen(act_one, x3_act)
     halo_finish(act_one, 3, x3_act)
 
     def keep_enc(rows, acc):

time: 101 us -> 98 us (0.970)
  Pallas kernels: 100 us -> 97.1 us
    pallas_call x1, Pallas kernels: 96 us -> 93 us  [on_device(): pl.pallas_call(kernel, out_shape=(jax.ShapeDtypeStruct(grid, BF16), jax.S...]
where the time goes in v10:
time: 98 us; the launch traced here: 97.9 us
  Pallas kernels  97.1 us (99%)
    pallas_call x1, Pallas kernels, on_device(): pl.pallas_call(kernel, out_shape=(jax.ShapeDtypeStruct(grid, BF16), jax.S...  93 us
    pallas_call x1, Pallas kernels, on_device(): pl.pallas_call(hand_over, out_shape=(jax.ShapeDtypeStruct(grid, BF16), ja...  4.08 us

profile of v10, /device:TPU:1, one launch (start us, length us, event | category | flops | bytes accessed | tf_op | source)
XLA Modules:
  0.0 97.9 jit_solution(2113789224196247511)
XLA Ops:
  0.6 93.0 %shard_map.111 = (bf16[16,128,256]{2,1,0:T(8,128)(2,1)}, bf16[64,2,32,128]{3,2,1,0:T(8,128)(2,1)}, bf16[2,3,2,768,128]{4,3,2,1,0:T(8,128)(2,1)}, f32[128,256]{1,0:T(8,128)}) custom-call(bf16[64,2,32,128]{3,2,1,0:T(8,128)(2,1)} %bitcast.11, s32[32,128]{1,0:T(8,128)} %bitcast.13, s32[32,128]{1,0:T(8,128)} %bitcast.14, s32[1,128]{1,0:T(1,128)} %live_counts.1, ...), custom_call_target="tpu_custom_call" | custom-call | flops 30000001024 | bytes 20000000 | tf_op jit(solution)/shard_map/pallas_call | solution.py:750
  93.6 4.1 %shard_map.112 = (bf16[16,128,256]{2,1,0:T(8,128)(2,1)}, bf16[64,2,32,128]{3,2,1,0:T(8,128)(2,1)}, f32[4608,256]{1,0:T(8,128)}, f32[128,256]{1,0:T(8,128)}) custom-call(bf16[16,128,256]{2,1,0:T(8,128)(2,1)} %get-tuple-element.12.enc_in, bf16[64,2,32,128]{3,2,1,0:T(8,128)(2,1)} %get-tuple-element.13.vg_in, bf16[2,4608,128]{2,1,0:T(8,128)(2,1)} %bitcast.8, ...), custom_call_target="tpu_custom_call" | custom-call | tf_op jit(solution)/shard_map/pallas_call | solution.py:777

commit v11 on v10

--- a/solution.py
+++ b/solution.py
@@ -311,8 +311,6 @@
     conv(x3_cot, 1, keep_back, flip=True)
     meta_wait(2)
 
-    placed[...] = jnp.zeros_like(placed)
-    counts[...] = jnp.zeros_like(counts)
     slot_mask = jnp.where(
         lax.rem(iota((CAP, 128), 1), 32) == iota((CAP, 128), 0), 1.0, 0.0
     ).astype(F32)
@@ -350,7 +348,8 @@
             both[0:COLS] == iota((COLS, GROUP), 0).astype(F32), 1.0, 0.0
         ).astype(BF16)
         rowl[...] = both[COLS : COLS + 16]
-        counts[...] += dot(colhot[...], rk[...])
+        tally = dot(colhot[...], rk[...])
+        counts[...] = tally if g == 0 else counts[...] + tally
 
         hot = colhot[...].reshape(8, 16, GROUP)
         for b in range(4):
@@ -359,7 +358,8 @@
                 mask = jnp.where(rowl[...] == float(r), 1.0, 0.0).astype(BF16)
                 rows.append((hot * mask[None]).reshape(COLS, GROUP))
             at = slice(b * 512, b * 512 + 512)
-            placed[at, :] += dot(jnp.concatenate(rows, axis=0), ew[...])
+            here = dot(jnp.concatenate(rows, axis=0), ew[...])
+            placed[at, :] = here if g == 0 else placed[at, :] + here
 
     kind = lax.rem(iota((256, CH), 0), 16)
     half_u, half_v = 2 * lax.div(kind, 4) + 1, 2 * lax.rem(kind, 4) + 1

time: 98 us -> 98 us (level)
  no operation moved by 1% of the time
where the time goes in v11:
time: 98 us; the launch traced here: 97.9 us
  Pallas kernels  97.1 us (99%)
    pallas_call x1, Pallas kernels, on_device(): pl.pallas_call(kernel, out_shape=(jax.ShapeDtypeStruct(grid, BF16), jax.S...  93 us
    pallas_call x1, Pallas kernels, on_device(): pl.pallas_call(hand_over, out_shape=(jax.ShapeDtypeStruct(grid, BF16), ja...  4.08 us

profile of v11, /device:TPU:1, one launch (start us, length us, event | category | flops | bytes accessed | tf_op | source)
XLA Modules:
  0.0 97.9 jit_solution(2113789224196247511)
XLA Ops:
  0.6 93.0 %shard_map.111 = (bf16[16,128,256]{2,1,0:T(8,128)(2,1)}, bf16[64,2,32,128]{3,2,1,0:T(8,128)(2,1)}, bf16[2,3,2,768,128]{4,3,2,1,0:T(8,128)(2,1)}, f32[128,256]{1,0:T(8,128)}) custom-call(bf16[64,2,32,128]{3,2,1,0:T(8,128)(2,1)} %bitcast.11, s32[32,128]{1,0:T(8,128)} %bitcast.13, s32[32,128]{1,0:T(8,128)} %bitcast.14, s32[1,128]{1,0:T(1,128)} %live_counts.1, ...), custom_call_target="tpu_custom_call" | custom-call | flops 30000001024 | bytes 20000000 | tf_op jit(solution)/shard_map/pallas_call | solution.py:750
  93.6 4.1 %shard_map.112 = (bf16[16,128,256]{2,1,0:T(8,128)(2,1)}, bf16[64,2,32,128]{3,2,1,0:T(8,128)(2,1)}, f32[4608,256]{1,0:T(8,128)}, f32[128,256]{1,0:T(8,128)}) custom-call(bf16[16,128,256]{2,1,0:T(8,128)(2,1)} %get-tuple-element.12.enc_in, bf16[64,2,32,128]{3,2,1,0:T(8,128)(2,1)} %get-tuple-element.13.vg_in, bf16[2,4608,128]{2,1,0:T(8,128)(2,1)} %bitcast.8, ...), custom_call_target="tpu_custom_call" | custom-call | tf_op jit(solution)/shard_map/pallas_call | solution.py:777
